TPU v7x, 32 devices: a whole 2x2x4 slice. The times are simulated.
32 devices in a mesh: grp: 2 (over core), aux: 4 (over y, x), orb: 4 (over z).
Axes of the slice: x: 2, y: 2, z: 4, core: 2. Of those that a mesh axis runs over, the one named last changes fastest.
Arguments:
- fitted_tensor: bfloat16 [4, 8192, 8192], P('grp', 'aux', 'orb'), may hold values from -0.23925781 to 0.23925781
- block_mask: int32 [2, 64, 64], P('grp'), may hold values 0 or 1
- orbitals: bfloat16 [8192, 256], P('aux'), may hold values from -0.0625 to 0.0625
- nuclear: float32 [8192], replicated, may hold values from 0.5 to 1.5
- centres: float32 [3, 8192], replicated, may hold values from 0 to 8
- mm_positions: float32 [3, 32768], P(None, ('grp', 'aux', 'orb')), may hold values from 0 to 8
- mm_charges: float32 [32768], P(('grp', 'aux', 'orb')), may hold values from -0.12 to 0.12
- neighbours: int32 [32, 2], P(('grp', 'aux', 'orb')), may hold values from 0 to 63, all different within a row
Outputs:
- fock: float32 [8192, 8192], P(('aux', 'orb'))
- mm_potential: float32 [32768], P(('grp', 'aux', 'orb'))
Inputs may be any that keep to these rules, and one draw needn't show every extreme that they name: `neighbours`: each row names 2 different blocks; every block is named by some row.
All inputs are finite; a program needn't handle non-finite values. No bound on the sum of `block_mask` on one device may be relied on, other than what follows from the above.
Results may differ from a plain program's by a relative error of at most 0.01.
Values may be sent and summed in bfloat16 or wider, within the bound.
A program may use at most 128 MiB of HBM per device.

v0:
```python
import functools

import jax
import jax.numpy as jnp
from jax import lax
from jax.experimental import pallas as pl
from jax.experimental.pallas import tpu as pltpu
from jax.sharding import PartitionSpec as P

BLK = 128
VMEM_LIMIT = 48 * 1024 * 1024

softening = 1.0


def near_kernel(picker, centre_blocks, atom_xyz):
    near_xyz = jnp.einsum("kb,cbj->ckj", picker, centre_blocks, precision=lax.Precision.HIGHEST)
    near_xyz = near_xyz.reshape(3, picker.shape[0] * centre_blocks.shape[2])
    offsets = near_xyz[:, :, None] - atom_xyz[:, None, :]
    return lax.rsqrt(jnp.sum(offsets * offsets, axis=0) + softening)


def products_kernel(t_ref, mask_ref, win_ref, c_ref, x_ref, dens_ref):
    parts, rows, cols = t_ref.shape
    row_mask = mask_ref[0]

    @pl.when(pl.program_id(0) == 0)
    def _():
        dens_ref[...] = jnp.zeros_like(dens_ref)

    own = c_ref[...].astype(jnp.float32)
    for p in range(parts):
        prod = jnp.dot(t_ref[p] * row_mask, win_ref[...], preferred_element_type=jnp.float32)
        x_ref[p] = prod.astype(x_ref.dtype)
        dens_ref[p] += jnp.sum((prod * own).reshape(rows // 8, 8, prod.shape[1]), axis=0)


def products_call(fitted, mask_rows, window_c, own_c):
    parts, rows, cols = fitted.shape
    nocc = window_c.shape[1]
    return pl.pallas_call(
        products_kernel,
        grid=(rows // BLK,),
        in_specs=[
            pl.BlockSpec((parts, BLK, cols), lambda i: (0, i, 0)),
            pl.BlockSpec((1, 1, cols), lambda i: (i, 0, 0)),
            pl.BlockSpec((cols, nocc), lambda i: (0, 0)),
            pl.BlockSpec((BLK, nocc), lambda i: (i, 0)),
        ],
        out_specs=[
            pl.BlockSpec((parts, BLK, nocc), lambda i: (0, i, 0)),
            pl.BlockSpec((parts, 8, nocc), lambda i: (0, 0, 0)),
        ],
        out_shape=[
            jax.ShapeDtypeStruct((parts, rows, nocc), jnp.bfloat16),
            jax.ShapeDtypeStruct((parts, 8, nocc), jnp.float32),
        ],
        compiler_params=pltpu.CompilerParams(vmem_limit_bytes=VMEM_LIMIT),
        cost_estimate=pl.CostEstimate(
            flops=2 * parts * rows * cols * nocc,
            bytes_accessed=2 * parts * rows * (cols + nocc),
            transcendentals=0,
        ),
        name="products",
    )(fitted, mask_rows, window_c, own_c)


def coulomb_kernel(place_ref, dens_ref, ta_ref, ma_ref, tk_ref, mk_ref, away_ref, kept_ref):
    for t_ref, mask_ref, out_ref in ((ta_ref, ma_ref, away_ref), (tk_ref, mk_ref, kept_ref)):
        total = t_ref[0].astype(jnp.float32) * dens_ref[0]
        for p in range(1, t_ref.shape[0]):
            total += t_ref[p].astype(jnp.float32) * dens_ref[p]
        out_ref[...] = (total * mask_ref[0].astype(jnp.float32)).astype(out_ref.dtype)


def coulomb_call(place, densities, fitted, mask_rows, half):
    parts, rows, cols = fitted.shape
    tile = min(BLK, half)
    steps = half // tile

    def away_tile(i, place_ref):
        return (place_ref[1] * 2 + 1 - place_ref[0]) * steps + i

    def kept_tile(i, place_ref):
        return (place_ref[1] * 2 + place_ref[0]) * steps + i

    def tensor_spec(which):
        return pl.BlockSpec((parts, tile, cols), lambda i, place_ref, d: (0, which(i, place_ref), 0))

    def mask_spec(which):
        return pl.BlockSpec(
            (1, 1, cols), lambda i, place_ref, d: (which(i, place_ref) * tile // BLK, 0, 0)
        )

    return pl.pallas_call(
        coulomb_kernel,
        grid_spec=pltpu.PrefetchScalarGridSpec(
            num_scalar_prefetch=2,
            grid=(steps,),
            in_specs=[
                tensor_spec(away_tile),
                mask_spec(away_tile),
                tensor_spec(kept_tile),
                mask_spec(kept_tile),
            ],
            out_specs=[pl.BlockSpec((tile, cols), lambda i, place_ref, d: (i, 0))] * 2,
        ),
        out_shape=[jax.ShapeDtypeStruct((half, cols), jnp.bfloat16)] * 2,
        compiler_params=pltpu.CompilerParams(vmem_limit_bytes=VMEM_LIMIT),
        cost_estimate=pl.CostEstimate(
            flops=4 * parts * half * cols,
            bytes_accessed=4 * half * cols * (parts + 1),
            transcendentals=0,
        ),
        name="coulomb",
    )(place, densities, fitted, mask_rows, fitted, mask_rows)


def fock_kernel(shifts, place_ref, own_ref, mate_ref, all_ref, mate_all_ref, field_ref, *refs):
    mine, theirs, out_ref = refs[:shifts], refs[shifts : 2 * shifts], refs[2 * shifts]
    parts = own_ref.shape[0]
    rows, cols = out_ref.shape
    half = rows // 2
    per_src = mine[0].shape[1] // cols
    dims = (((1,), (1,)), ((), ()))
    grp_id, row0, orb_id = place_ref[0], place_ref[1], place_ref[2]

    def slab(a, b):
        total = lax.dot_general(a[0], b[0], dims, preferred_element_type=jnp.float32)
        for p in range(1, parts):
            total += lax.dot_general(a[p], b[p], dims, preferred_element_type=jnp.float32)
        return total

    out_ref[...] = -0.5 * (slab(own_ref, all_ref) + slab(mate_ref, mate_all_ref))

    step = pl.program_id(0)
    shift = lax.rem(orb_id - step // per_src + shifts, shifts)
    col_in = pl.multiple_of(lax.rem(step, per_src) * cols, cols)
    own_row = pl.multiple_of(grp_id * half, half)
    mate_row = pl.multiple_of((1 - grp_id) * half, half)
    for k in range(shifts):

        @pl.when(shift == k)
        def _():
            out_ref[pl.ds(own_row, half), :] += mine[k][:, pl.ds(col_in, cols)].astype(jnp.float32)
            out_ref[pl.ds(mate_row, half), :] += theirs[k][:, pl.ds(col_in, cols)].astype(jnp.float32)

    col0 = step * cols

    @pl.when((row0 < col0 + cols) & (row0 + rows > col0))
    def _():
        row_ids = row0 + lax.broadcasted_iota(jnp.int32, (rows, cols), 0)
        col_ids = col0 + lax.broadcasted_iota(jnp.int32, (rows, cols), 1)
        out_ref[...] += jnp.where(row_ids == col_ids, field_ref[...], jnp.float32(0.0))


def fock_call(place, x_own, x_mate, x_all, x_mate_all, field_col, mine, theirs):
    parts, rows, nocc = x_own.shape
    total = x_all.shape[1]
    half, per_src = mine[0].shape
    cols = min(1024, per_src)
    own_spec = pl.BlockSpec((parts, rows, nocc), lambda j: (0, 0, 0))
    all_spec = pl.BlockSpec((parts, cols, nocc), lambda j: (0, j, 0))
    return pl.pallas_call(
        functools.partial(fock_kernel, len(mine)),
        grid=(total // cols,),
        in_specs=[
            pl.BlockSpec(memory_space=pltpu.SMEM),
            own_spec,
            own_spec,
            all_spec,
            all_spec,
            pl.BlockSpec((rows, 1), lambda j: (0, 0)),
        ]
        + [pl.BlockSpec((half, per_src), lambda j: (0, 0))] * (2 * len(mine)),
        out_specs=pl.BlockSpec((rows, cols), lambda j: (0, j)),
        out_shape=jax.ShapeDtypeStruct((rows, total), jnp.float32),
        compiler_params=pltpu.CompilerParams(vmem_limit_bytes=VMEM_LIMIT),
        cost_estimate=pl.CostEstimate(
            flops=4 * parts * rows * total * nocc,
            bytes_accessed=4 * parts * total * nocc + 4 * rows * total + 2 * rows * total,
            transcendentals=0,
        ),
        name="fock",
    )(place, x_own, x_mate, x_all, x_mate_all, field_col, *mine, *theirs)


def swap(value):
    return lax.ppermute(value, "grp", [(0, 1), (1, 0)])


def per_device(
    fitted_tensor, block_mask, orbitals, nuclear, centres, mm_positions, mm_charges, neighbours
):
    parts, row_span, col_span = fitted_tensor.shape
    nocc = orbitals.shape[1]
    orb_count = lax.axis_size("orb")
    aux_count = lax.axis_size("aux")
    grp_count = lax.axis_size("grp")
    grp_id = lax.axis_index("grp")
    aux_id = lax.axis_index("aux")
    orb_id = lax.axis_index("orb")
    own_span = row_span // orb_count
    half = own_span // 2
    block_total = block_mask.shape[1]
    row_start = aux_id * row_span
    col_start = orb_id * col_span

    if aux_count == orb_count:
        perm = [
            (a * orb_count + o, o * orb_count + a)
            for a in range(aux_count)
            for o in range(orb_count)
        ]
        c_half = lax.dynamic_slice_in_dim(orbitals, grp_id * (row_span // 2), row_span // 2, 0)
        c_half = lax.ppermute(c_half, ("aux", "orb"), perm)
        c_mate = swap(c_half)
        window_c = jnp.where(
            grp_id == 0, jnp.stack([c_half, c_mate]), jnp.stack([c_mate, c_half])
        ).reshape(col_span, nocc)
    else:
        whole_c = lax.all_gather(orbitals, "aux", axis=0, tiled=True)
        window_c = lax.dynamic_slice_in_dim(whole_c, col_start, col_span, 0)

    bits = lax.dynamic_slice(
        block_mask[0],
        (row_start // BLK, col_start // BLK),
        (row_span // BLK, col_span // BLK),
    ).astype(jnp.bfloat16)
    mask_rows = jnp.repeat(bits, BLK, axis=1)[:, None, :]

    own_float = orbitals.astype(jnp.float32)
    own_population = 2.0 * jnp.sum(own_float * own_float, axis=1)
    population = lax.all_gather(own_population, "aux", axis=0, tiled=True)
    centre_blocks = centres.reshape(3, block_total, BLK)
    picker = (neighbours[0][:, None] == jnp.arange(block_total, dtype=jnp.int32)[None, :]).astype(
        jnp.float32
    )
    kernel = near_kernel(picker, centre_blocks, mm_positions)
    contrib = jnp.dot(kernel, mm_charges, precision=lax.Precision.HIGHEST).reshape(
        picker.shape[0], BLK
    )
    field_part = jnp.dot(picker.T, contrib, precision=lax.Precision.HIGHEST)

    window_c, population = lax.optimization_barrier((window_c, population))
    qm_charge = nuclear - population
    charge_blocks = qm_charge.reshape(block_total, BLK)
    near_q = jnp.dot(picker, charge_blocks, precision=lax.Precision.HIGHEST).reshape(-1)
    mm_potential = jnp.dot(near_q, kernel, precision=lax.Precision.HIGHEST)

    x_part, dens_lanes = products_call(fitted_tensor, mask_rows, window_c, orbitals)
    dens_part = 2.0 * jnp.sum(dens_lanes, axis=(1, 2))
    dens_slots = jnp.zeros((grp_count, BLK), jnp.float32)
    dens_slots = lax.dynamic_update_slice(dens_slots, dens_part[None, :], (grp_id, 0))
    sums = lax.psum(jnp.concatenate([field_part, dens_slots], axis=0), ("grp", "aux", "orb"))

    x_blocks = x_part.reshape(parts, orb_count, own_span, nocc)
    targets = [lax.rem(orb_id + k, orb_count) for k in range(orb_count)]
    moves = [[(s, (s + k) % orb_count) for s in range(orb_count)] for k in range(orb_count)]
    arrived = []
    for k in range(1, orb_count):
        block = lax.dynamic_index_in_dim(x_blocks, targets[k], 1, keepdims=False)
        arrived.append(lax.ppermute(block, "orb", moves[k]))
    sums, *arrived = lax.optimization_barrier((sums, *arrived))
    field_vec = sums[:block_total].reshape(-1)
    densities = lax.dynamic_slice(sums, (block_total + grp_id, 0), (1, parts))[0]
    x_sum = lax.dynamic_index_in_dim(x_blocks, orb_id, 1, keepdims=False).astype(jnp.float32)
    for block in arrived:
        x_sum += block.astype(jnp.float32)
    x_own = x_sum.astype(jnp.bfloat16)
    x_mate = swap(x_own)
    x_all = lax.all_gather(x_own, ("aux", "orb"), axis=1, tiled=True)

    mine = [None] * orb_count
    for k in list(range(1, orb_count)) + [0]:
        at = jnp.stack([grp_id, targets[k]]).astype(jnp.int32)
        away, kept = coulomb_call(at, densities, fitted_tensor, mask_rows, half)
        both = (kept.astype(jnp.float32) + swap(away).astype(jnp.float32)).astype(jnp.bfloat16)
        mine[k] = lax.ppermute(both, "orb", moves[k]) if k else both
    x_all, *mine = lax.optimization_barrier((x_all, *mine))
    theirs = [swap(block) for block in mine]
    x_mate_all = swap(x_all)

    own_first = row_start + orb_id * own_span
    field_col = lax.dynamic_slice_in_dim(field_vec, own_first, own_span, 0)[:, None]
    place = jnp.stack([grp_id, own_first, orb_id]).astype(jnp.int32)
    fock = fock_call(place, x_own, x_mate, x_all, x_mate_all, field_col, mine, theirs)
    return (fock, mm_potential)


def solution(mesh):
    in_specs = (
        P("grp", "aux", "orb"),
        P("grp", None, None),
        P("aux", None),
        P(),
        P(),
        P(None, ("grp", "aux", "orb")),
        P(("grp", "aux", "orb")),
        P(("grp", "aux", "orb"), None),
    )
    out_specs = (P(("aux", "orb"), None), P(("grp", "aux", "orb")))
    return jax.shard_map(
        per_device, mesh=mesh, in_specs=in_specs, out_specs=out_specs, check_vma=False
    )
```

profile of v0, /device:TPU:0, one launch (start us, length us, event | category | flops | bytes accessed | tf_op | source)
XLA Modules:
  0.0 375.9 jit_solution(6270436667691109960)
XLA Ops:
  7.2 0.0 copy-start
  7.2 0.0 all-gather.2.cloned.1.call-start
  7.2 1.1 constant_dynamic-slice_fusion.1
  8.3 0.7 collective-permute-start
  9.1 1.1 convolution_bitcast_fusion
  10.2 1.6 multiply_reduce_fusion.1
  11.8 0.5 collective-permute-start.1
  12.3 0.8 fusion.12
  13.1 0.1 broadcast_in_dim.12
  13.3 44.5 %all_gather.6 = f32[8192]{0:T(1024)S(1)} all-gather(f32[2048]{0:T(1024)S(1)} %broadcast_multiply_fusion), channel_id=1, replica_groups=mesh['grp'=2,'aux'=4,'orb'=4] {'aux'}, dimensions={0}, use_global_device_ids=true | all-gather | bytes 40960 | tf_op jit(solution)/shard_map/all_gather | solution.py:234
  57.8 0.0 copy-start.2
  57.8 0.4 multiply_reduce_fusion
  58.2 1.0 fusion.4
  59.2 0.0 copy-done.6
  59.2 0.2 maximum_select_fusion
  59.4 14.7 %products.1 = (bf16[2,2048,256]{2,1,0:T(8,128)(2,1)S(1)}, f32[2,8,256]{2,1,0:T(8,128)S(1)}) custom-call(bf16[2,2048,2048]{2,1,0:T(8,128)(2,1)} %tk_ref.7, bf16[16,1,2048]{2,1,0:T(2,128)(2,1)S(1)} %broadcast_in_dim_reshape.5.mask_ref.ma_ref.mk_ref, bf16[2048,256]{1,0:T(8,128)(2,1)S(1)} %bitcast.60, bf16[2048,256]{1,0:T(8,128)(2,1)S(1)} %copy-done.2), custom_call_target="tpu_custom_call" | custom-call | flops 4294967296 | bytes 18874368 | tf_op jit(solution)/shard_map/products/pallas_call | solution.py:41
  74.1 0.0 copy-start.9
  74.1 0.9 dynamic-slice_bitcast_fusion
  75.0 3.6 collective-permute-start.4
  78.7 0.6 collective-permute-start.2
  79.2 0.3 fusion.14
  79.5 0.1 reduce_sum.29
  79.6 0.2 dynamic_update_slice.3
  79.8 63.9 %psum.7 = f32[66,128]{1,0:T(8,128)S(1)} all-reduce(f32[66,128]{1,0:T(8,128)S(1)} %pad_maximum_fusion), channel_id=1, replica_groups=mesh['grp'=2,'aux'=4,'orb'=4] {'grp','aux','orb'}, use_global_device_ids=true, to_apply=%region_3.4 | all-reduce | flops 8448 | bytes 67584 | tf_op jit(solution)/shard_map/psum | solution.py:255
  143.8 2.4 fusion.2.own_ref
  146.2 0.0 all-gather.2.cloned.1.call-update
  146.2 0.1 pad_add_fusion.4.place_ref
  146.3 3.2 coulomb.7
  149.5 0.1 collective-permute-start.11
  149.6 0.1 pad_add_fusion.2
  149.7 3.8 %coulomb.6 = (bf16[256,2048]{1,0:T(8,128)(2,1)}, bf16[256,2048]{1,0:T(8,128)(2,1)S(1)}) custom-call(s32[2]{0:T(128)S(1)} %get-tuple-element.48.place_ref, f32[2]{0:T(128)S(1)} %fusion.15.dens_ref, bf16[2,2048,2048]{2,1,0:T(8,128)(2,1)} %tk_ref.7, bf16[16,1,2048]{2,1,0:T(2,128)(2,1)S(1)} %broadcast_in_dim_reshape.5.mask_ref.ma_ref.mk_ref, ...), custom_call_target="tpu_custom_call" | custom-call | flops 4194304 | bytes 6291456 | tf_op jit(solution)/shard_map/coulomb/pallas_call | solution.py:95
  153.5 1.0 copy-done.4
  154.5 0.5 collective-permute-start.9
  155.0 0.1 pad_add_fusion.1.place_ref
  155.0 3.2 coulomb.5
  158.3 0.1 collective-permute-start.7
  158.4 3.2 coulomb.4
  161.6 0.6 collective-permute-start.6
  162.2 0.4 add_convert_fusion
  162.6 1.8 collective-permute-start.12
  164.3 1.6 add_convert_fusion.1
  166.0 0.1 collective-permute-start.10
  166.1 0.4 add_convert_fusion.2
  166.5 0.0 copy-start.7
  166.5 1.0 collective-permute-start.8
  167.5 0.4 add_convert_fusion.3.refs_0_
  167.9 23.7 %collective-permute-done.12.refs_3_ = bf16[256,2048]{1,0:T(8,128)(2,1)S(1)} collective-permute-done((bf16[256,2048]{1,0:T(8,128)(2,1)S(1)}, bf16[256,2048]{1,0:T(8,128)(2,1)S(1)}, u32[]{:S(2)}, u32[]{:S(2)}) %collective-permute-start.12) | collective-permute-done | bytes 1048608 | tf_op jit(solution)/shard_map/ppermute | solution.py:279
  191.6 102.1 %collective-permute-done.10.refs_2_ = bf16[256,2048]{1,0:T(8,128)(2,1)} collective-permute-done((bf16[256,2048]{1,0:T(8,128)(2,1)S(1)}, bf16[256,2048]{1,0:T(8,128)(2,1)}, u32[]{:S(2)}, u32[]{:S(2)}) %collective-permute-start.10) | collective-permute-done | bytes 1048608 | tf_op jit(solution)/shard_map/ppermute | solution.py:279
  293.7 34.7 %all-gather.2.cloned.1.call-done.all_ref = bf16[2,8192,256]{2,1,0:T(8,128)(2,1)} async-done(((bf16[2,512,256]{2,1,0:T(8,128)(2,1)}), bf16[2,8192,256]{2,1,0:T(8,128)(2,1)}) %all-gather.2.cloned.1.call-update) | async-done | bytes 8388624 | tf_op jit(solution)/shard_map/all_gather | solution.py:272
  328.4 0.1 collective-permute-start.13
  328.5 0.5 collective-permute-start.5
  328.9 0.1 collective-permute-start.14
  329.0 0.5 collective-permute-start.15
  329.4 0.1 collective-permute-start.16
  329.5 6.1 %collective-permute-done.5.mate_ref = bf16[2,512,256]{2,1,0:T(8,128)(2,1)S(1)} collective-permute-done((bf16[2,512,256]{2,1,0:T(8,128)(2,1)S(1)}, bf16[2,512,256]{2,1,0:T(8,128)(2,1)S(1)}, u32[]{:S(2)}, u32[]{:S(2)}) %collective-permute-start.5) | collective-permute-done | bytes 524320 | tf_op jit(solution)/shard_map/ppermute | solution.py:189
  335.6 0.4 collective-permute-start.17
  336.0 0.1 pad_add_fusion.place_ref
  336.0 0.2 fusion.9
  336.2 2.5 fusion.3
  338.7 0.1 dynamic_slice.32
  338.8 0.1 copy.42.field_ref
  339.0 8.2 %collective-permute-done.15.refs_5_ = bf16[256,2048]{1,0:T(8,128)(2,1)} collective-permute-done((bf16[256,2048]{1,0:T(8,128)(2,1)}, bf16[256,2048]{1,0:T(8,128)(2,1)}, u32[]{:S(2)}, u32[]{:S(2)}) %collective-permute-start.15) | collective-permute-done | bytes 1048608 | tf_op jit(solution)/shard_map/ppermute | solution.py:189
  347.1 1.5 collective-permute-done.16.refs_6_
  348.7 20.4 %fock.1 = f32[512,8192]{1,0:T(8,128)} custom-call(s32[3]{0:T(128)S(1)} %pad_add_fusion.place_ref, bf16[2,512,256]{2,1,0:T(8,128)(2,1)S(1)} %copy-done.3, bf16[2,512,256]{2,1,0:T(8,128)(2,1)S(1)} %collective-permute-done.5.mate_ref, bf16[2,8192,256]{2,1,0:T(8,128)(2,1)} %all-gather.2.cloned.1.call-done.all_ref, ...), custom_call_target="tpu_custom_call" | custom-call | flops 8589934592 | bytes 41943040 | tf_op jit(solution)/shard_map/fock/pallas_call | solution.py:164
  (36 shorter events, 0.1 us)
Async XLA Ops:
  7.2 51.0 %copy-start = (f32[1024]{0:T(1024)S(1)}, f32[1024]{0:T(1024)}, u32[]{:S(2)}) copy-start(f32[1024]{0:T(1024)} %param.14) | copy-start | bytes 12292
  7.2 50.6 %copy-start.8 = (f32[3,1024]{1,0:T(4,128)S(1)}, f32[3,1024]{1,0:T(4,128)}, u32[]{:S(2)}) copy-start(f32[3,1024]{1,0:T(4,128)} %param.13) | copy-start | bytes 36868
  7.2 321.2 %all-gather.2.cloned.1.call-start = ((), (), s32[]{:S(2)}) async-start(), calls=%async_computation | async-start | bytes 8912896 | tf_op jit(solution)/shard_map/all_gather | solution.py:272
  8.3 3.5 collective-permute-start
  11.8 47.3 %collective-permute-start.1 = (bf16[1024,256]{1,0:T(8,128)(2,1)S(1)}, bf16[1024,256]{1,0:T(8,128)(2,1)S(1)}, u32[]{:S(2)}, u32[]{:S(2)}) collective-permute-start(bf16[1024,256]{1,0:T(8,128)(2,1)S(1)} %collective-permute-done), channel_id=1, source_target_pairs={{0,16},{16,0},{1,17},{17,1},{2,18},{18,2},{3,19},{19,3},{4,20},{20... | collective-permute-start | bytes 1572872 | tf_op jit(solution)/shard_map/ppermute | solution.py:189
  57.8 1.6 copy-start.2
  58.2 1.0 copy-start.6
  74.1 5.1 %copy-start.9 = (s32[1,2]{1,0:T(1,128)S(1)}, s32[1,2]{1,0:T(1,128)}, u32[]{:S(2)}) copy-start(s32[1,2]{1,0:T(1,128)} %param.15) | copy-start | bytes 28
  75.0 68.7 %collective-permute-start.4 = (bf16[2,512,256]{2,1,0:T(8,128)(2,1)}, bf16[2,512,256]{2,1,0:T(8,128)(2,1)}, u32[]{:S(2)}, u32[]{:S(2)}) collective-permute-start(bf16[2,512,256]{2,1,0:T(8,128)(2,1)} %get-tuple-element.44), channel_id=1, source_target_pairs={{0,3},{1,0},{2,1},{3,2},{4,7},{5,4},{6,5},{7,6},{8,11},{9,8},{10,9... | collective-permute-start | bytes 1572872 | tf_op jit(solution)/shard_map/ppermute | solution.py:263
  78.7 65.1 %collective-permute-start.3 = (bf16[2,512,256]{2,1,0:T(8,128)(2,1)S(1)}, bf16[2,512,256]{2,1,0:T(8,128)(2,1)}, u32[]{:S(2)}, u32[]{:S(2)}) collective-permute-start(bf16[2,512,256]{2,1,0:T(8,128)(2,1)S(1)} %get-tuple-element.45), channel_id=1, source_target_pairs={{0,2},{1,3},{2,0},{3,1},{4,6},{5,7},{6,4},{7,5},{8,10},{9,11},{10,... | collective-permute-start | bytes 1572872 | tf_op jit(solution)/shard_map/ppermute | solution.py:263
  78.7 65.1 %collective-permute-start.2 = (bf16[2,512,256]{2,1,0:T(8,128)(2,1)S(1)}, bf16[2,512,256]{2,1,0:T(8,128)(2,1)}, u32[]{:S(2)}, u32[]{:S(2)}) collective-permute-start(bf16[2,512,256]{2,1,0:T(8,128)(2,1)S(1)} %get-tuple-element.46), channel_id=1, source_target_pairs={{0,1},{1,2},{2,3},{3,0},{4,5},{5,6},{6,7},{7,4},{8,9},{9,10},{10,1... | collective-permute-start | bytes 1572872 | tf_op jit(solution)/shard_map/ppermute | solution.py:263
  149.5 12.6 %collective-permute-start.11 = (bf16[256,2048]{1,0:T(8,128)(2,1)S(1)}, bf16[256,2048]{1,0:T(8,128)(2,1)S(1)}, u32[]{:S(2)}, u32[]{:S(2)}) collective-permute-start(bf16[256,2048]{1,0:T(8,128)(2,1)S(1)} %get-tuple-element.37), channel_id=1, source_target_pairs={{0,16},{16,0},{1,17},{17,1},{2,18},{18,2},{3,19},{19,3},{4,20},{20... | collective-permute-start | bytes 3145736 | tf_op jit(solution)/shard_map/ppermute | solution.py:189
  153.5 1.0 copy-start.4
  154.5 9.9 %collective-permute-start.9 = (bf16[256,2048]{1,0:T(8,128)(2,1)}, bf16[256,2048]{1,0:T(8,128)(2,1)}, u32[]{:S(2)}, u32[]{:S(2)}) collective-permute-start(bf16[256,2048]{1,0:T(8,128)(2,1)} %get-tuple-element.35), channel_id=1, source_target_pairs={{0,16},{16,0},{1,17},{17,1},{2,18},{18,2},{3,19},{19,3},{4,20},{20... | collective-permute-start | bytes 3145736 | tf_op jit(solution)/shard_map/ppermute | solution.py:189
  158.3 7.8 %collective-permute-start.7 = (bf16[256,2048]{1,0:T(8,128)(2,1)S(1)}, bf16[256,2048]{1,0:T(8,128)(2,1)S(1)}, u32[]{:S(2)}, u32[]{:S(2)}) collective-permute-start(bf16[256,2048]{1,0:T(8,128)(2,1)S(1)} %get-tuple-element.33), channel_id=1, source_target_pairs={{0,16},{16,0},{1,17},{17,1},{2,18},{18,2},{3,19},{19,3},{4,20},{20... | collective-permute-start | bytes 3145736 | tf_op jit(solution)/shard_map/ppermute | solution.py:189
  161.6 2.7 copy-start.5
  161.6 5.8 %collective-permute-start.6 = (bf16[256,2048]{1,0:T(8,128)(2,1)S(1)}, bf16[256,2048]{1,0:T(8,128)(2,1)S(1)}, u32[]{:S(2)}, u32[]{:S(2)}) collective-permute-start(bf16[256,2048]{1,0:T(8,128)(2,1)S(1)} %get-tuple-element.31), channel_id=1, source_target_pairs={{0,16},{16,0},{1,17},{17,1},{2,18},{18,2},{3,19},{19,3},{4,20},{20... | collective-permute-start | bytes 3145736 | tf_op jit(solution)/shard_map/ppermute | solution.py:189
  162.6 29.0 %collective-permute-start.12 = (bf16[256,2048]{1,0:T(8,128)(2,1)S(1)}, bf16[256,2048]{1,0:T(8,128)(2,1)S(1)}, u32[]{:S(2)}, u32[]{:S(2)}) collective-permute-start(bf16[256,2048]{1,0:T(8,128)(2,1)S(1)} %add_convert_fusion), channel_id=1, source_target_pairs={{0,3},{1,0},{2,1},{3,2},{4,7},{5,4},{6,5},{7,6},{8,11},{9,8},{10,9... | collective-permute-start | bytes 3145736 | tf_op jit(solution)/shard_map/ppermute | solution.py:279
  166.0 127.7 %collective-permute-start.10 = (bf16[256,2048]{1,0:T(8,128)(2,1)S(1)}, bf16[256,2048]{1,0:T(8,128)(2,1)}, u32[]{:S(2)}, u32[]{:S(2)}) collective-permute-start(bf16[256,2048]{1,0:T(8,128)(2,1)S(1)} %add_convert_fusion.1), channel_id=1, source_target_pairs={{0,2},{1,3},{2,0},{3,1},{4,6},{5,7},{6,4},{7,5},{8,10},{9,11},{10,... | collective-permute-start | bytes 3145736 | tf_op jit(solution)/shard_map/ppermute | solution.py:279
  166.5 162.0 %copy-start.3 = (bf16[2,512,256]{2,1,0:T(8,128)(2,1)S(1)}, bf16[2,512,256]{2,1,0:T(8,128)(2,1)}, u32[]{:S(2)}) copy-start(bf16[2,512,256]{2,1,0:T(8,128)(2,1)} %fusion.2.own_ref) | copy-start | bytes 1572868
  166.5 169.6 %copy-start.7 = (f32[8192]{0:T(1024)S(1)}, f32[8192]{0:T(1024)}, u32[]{:S(2)}) copy-start(f32[8192]{0:T(1024)} %param.11) | copy-start | bytes 98308
  166.5 127.2 %collective-permute-start.8 = (bf16[256,2048]{1,0:T(8,128)(2,1)S(1)}, bf16[256,2048]{1,0:T(8,128)(2,1)}, u32[]{:S(2)}, u32[]{:S(2)}) collective-permute-start(bf16[256,2048]{1,0:T(8,128)(2,1)S(1)} %add_convert_fusion.2), channel_id=1, source_target_pairs={{0,1},{1,2},{2,3},{3,0},{4,5},{5,6},{6,7},{7,4},{8,9},{9,10},{10,1... | collective-permute-start | bytes 3145736 | tf_op jit(solution)/shard_map/ppermute | solution.py:279
  328.4 20.3 %collective-permute-start.13 = (bf16[2,8192,256]{2,1,0:T(8,128)(2,1)}, bf16[2,8192,256]{2,1,0:T(8,128)(2,1)}, u32[]{:S(2)}, u32[]{:S(2)}) collective-permute-start(bf16[2,8192,256]{2,1,0:T(8,128)(2,1)} %all-gather.2.cloned.1.call-done.all_ref), channel_id=1, source_target_pairs={{0,16},{16,0},{1,17},{17,1},{2,18},{18,2},{3,19},{19,3},{4,20},{20... | collective-permute-start | bytes 25165832 | tf_op jit(solution)/shard_map/ppermute | solution.py:189
  328.5 7.1 %collective-permute-start.5 = (bf16[2,512,256]{2,1,0:T(8,128)(2,1)S(1)}, bf16[2,512,256]{2,1,0:T(8,128)(2,1)S(1)}, u32[]{:S(2)}, u32[]{:S(2)}) collective-permute-start(bf16[2,512,256]{2,1,0:T(8,128)(2,1)S(1)} %copy-done.3), channel_id=1, source_target_pairs={{0,16},{16,0},{1,17},{17,1},{2,18},{18,2},{3,19},{19,3},{4,20},{20... | collective-permute-start | bytes 1572872 | tf_op jit(solution)/shard_map/ppermute | solution.py:189
  328.9 10.0 %collective-permute-start.14 = (bf16[256,2048]{1,0:T(8,128)(2,1)S(1)}, bf16[256,2048]{1,0:T(8,128)(2,1)}, u32[]{:S(2)}, u32[]{:S(2)}) collective-permute-start(bf16[256,2048]{1,0:T(8,128)(2,1)S(1)} %add_convert_fusion.3.refs_0_), channel_id=1, source_target_pairs={{0,16},{16,0},{1,17},{17,1},{2,18},{18,2},{3,19},{19,3},{4,20},{20... | collective-permute-start | bytes 3145736 | tf_op jit(solution)/shard_map/ppermute | solution.py:189
  329.0 18.2 %collective-permute-start.15 = (bf16[256,2048]{1,0:T(8,128)(2,1)}, bf16[256,2048]{1,0:T(8,128)(2,1)}, u32[]{:S(2)}, u32[]{:S(2)}) collective-permute-start(bf16[256,2048]{1,0:T(8,128)(2,1)} %collective-permute-done.8.refs_1_), channel_id=1, source_target_pairs={{0,16},{16,0},{1,17},{17,1},{2,18},{18,2},{3,19},{19,3},{4,20},{20... | collective-permute-start | bytes 3145736 | tf_op jit(solution)/shard_map/ppermute | solution.py:189
  329.4 19.2 %collective-permute-start.16 = (bf16[256,2048]{1,0:T(8,128)(2,1)}, bf16[256,2048]{1,0:T(8,128)(2,1)}, u32[]{:S(2)}, u32[]{:S(2)}) collective-permute-start(bf16[256,2048]{1,0:T(8,128)(2,1)} %collective-permute-done.10.refs_2_), channel_id=1, source_target_pairs={{0,16},{16,0},{1,17},{17,1},{2,18},{18,2},{3,19},{19,3},{4,20},{20... | collective-permute-start | bytes 3145736 | tf_op jit(solution)/shard_map/ppermute | solution.py:189
  335.6 13.1 %collective-permute-start.17 = (bf16[256,2048]{1,0:T(8,128)(2,1)S(1)}, bf16[256,2048]{1,0:T(8,128)(2,1)}, u32[]{:S(2)}, u32[]{:S(2)}) collective-permute-start(bf16[256,2048]{1,0:T(8,128)(2,1)S(1)} %collective-permute-done.12.refs_3_), channel_id=1, source_target_pairs={{0,16},{16,0},{1,17},{17,1},{2,18},{18,2},{3,19},{19,3},{4,20},{20... | collective-permute-start | bytes 3145736 | tf_op jit(solution)/shard_map/ppermute | solution.py:189
  348.7 20.4 %copy-start.1 = (f32[1024]{0:T(1024)S(1)}, f32[1024]{0:T(1024)}, u32[]{:S(2)}) copy-start(f32[1024]{0:T(1024)} %param.14) | copy-start | bytes 12292
Sparse Core Ops, SparseCore 0:
  146.3 182.0 all-gather.1
where the time goes:
time: 377 us; the launch traced here: 376 us
  waiting for transfers between devices  176 us (47%)
  blocking collectives  108 us (29%)
  Pallas kernels  48.6 us (13%)
  between operations  14.4 us (4%)
  starting transfers between devices  10.9 us (3%)
  other arithmetic  8.52 us (2%)
  matrix products  5.04 us (1%)
    ppermute x3, waiting for transfers between devices, per_device(): mine[k] = lax.ppermute(both, 'orb', moves[k]) if k else both  126 us
    psum x1, blocking collectives, per_device(): lax.psum(jnp.concatenate([field_part, dens_slots], axis=0), ('grp', 'aux'...  63.9 us
    all_gather x1, blocking collectives, per_device(): population = lax.all_gather(own_population, 'aux', axis=0, tiled=True)  44.5 us
    all_gather x1, waiting for transfers between devices, per_device(): x_all = lax.all_gather(x_own, ('aux', 'orb'), axis=1, tiled=True)  34.7 us
    pallas_call x1, Pallas kernels, fock_call(): pl.pallas_call(functools.partial(fock_kernel, len(mine)), grid=(total //...  20.4 us
    ppermute x11, waiting for transfers between devices, swap(): return lax.ppermute(value, 'grp', [(0, 1), (1, 0)])  15.8 us
    pallas_call x1, Pallas kernels, products_call(): pl.pallas_call(products_kernel, grid=(rows // BLK,), in_specs=[pl.BlockSp...  14.7 us
    pallas_call x4, Pallas kernels, coulomb_call(): pl.pallas_call(coulomb_kernel, grid_spec=pltpu.PrefetchScalarGridSpec(num...  13.5 us
  transfers between devices with their start and end apart: 19, of which 6 were waited for; matrix products, arithmetic and copies ran while one was open for 3% of the time, Pallas kernels for 4%

commit v1 on v0

--- a/solution.py
+++ b/solution.py
@@ -288,6 +288,554 @@
     return (fock, mm_potential)
 
 
+MESH = pl.DeviceIdType.MESH
+CHUNKS = 8
+GRID_VMEM = 58 * 1024 * 1024
+
+
+def grid_kernel(
+    t_hbm, mask_ref, c_ref, small_ref, out_ref, sums_ref,
+    t_ref, cw_ref, xp_ref, ra_ref, rb_ref, xa_ref, xm_ref, xo_ref, mr_ref, cr_ref, eb_ref,
+    s_ref, sr_ref, dens_ref,
+    t_sem, c_send, c_recv, ra_send, ra_recv, rb_send, rb_recv, xe_send, xe_recv,
+    pl_send, pl_recv, xm_send, xm_recv, xo_send, xo_recv, s_send, s_recv,
+    mr_send, mr_recv, cr_send, cr_recv, om_send, om_recv, ol_sem,
+):
+    parts, rows, cols = t_ref.shape
+    nocc = c_ref.shape[1]
+    chunk = rows // CHUNKS
+    own = rows // 4
+    half = cols // 2
+    quarter = cols // 4
+    per = CHUNKS // 2
+    g, a, z = lax.axis_index("grp"), lax.axis_index("aux"), lax.axis_index("orb")
+    mate = (1 - g, a, z)
+    is_mid = (z == 1) | (z == 2)
+    is_end = (z == 0) | (z == 3)
+    inner = jnp.where(z == 0, 1, 2)
+    outer = jnp.where(z == 1, 0, 3)
+    rel = lax.bitwise_xor(a, z)
+
+    def plane(k):
+        return (g, lax.bitwise_xor(a, k), z)
+
+    def remote(src, dst, send, recv, device):
+        return pltpu.make_async_remote_copy(
+            src_ref=src, dst_ref=dst, send_sem=send, recv_sem=recv,
+            device_id=device, device_id_type=MESH,
+        )
+
+    def t_copy(c):
+        span = pl.ds(c * chunk, chunk)
+        return pltpu.make_async_copy(t_hbm.at[:, span], t_ref.at[:, span], t_sem.at[c])
+
+    for c in range(CHUNKS):
+        t_copy(c).start()
+
+    barrier = pltpu.get_barrier_semaphore()
+    for peer in (
+        mate, plane(1), plane(2), plane(3),
+        (g, a, lax.rem(z + 1, 4)), (g, a, lax.rem(z + 2, 4)), (g, a, lax.rem(z + 3, 4)),
+    ):
+        pl.semaphore_signal(barrier, inc=1, device_id=peer, device_id_type=MESH)
+    pl.semaphore_wait(barrier, 7)
+
+    def quarter_copy(src_ref, q, slot, device):
+        span = pl.ds(pl.multiple_of(q * quarter, quarter), quarter)
+        return remote(src_ref.at[span], cw_ref.at[span], c_send.at[slot], c_recv.at[q], device)
+
+    first, second = 2 * g, 2 * g + 1
+
+    @pl.when(rel == 0)
+    def _():
+        quarter_copy(c_ref, first, 0, plane(1)).start()
+        quarter_copy(c_ref, second, 1, plane(2)).start()
+        quarter_copy(c_ref, second, 2, plane(1)).start()
+        quarter_copy(c_ref, first, 3, plane(2)).start()
+        cw_ref[...] = c_ref[...]
+
+    @pl.when(rel != 0)
+    def _():
+        for rank in range(2):
+            q = jnp.where(rel == 2, 2 * g + 1 - rank, 2 * g + rank)
+            quarter_copy(cw_ref, q, 0, mate).wait_recv()
+            if rank == 0:
+
+                @pl.when(rel == 1)
+                def _():
+                    quarter_copy(cw_ref, q, 2, plane(2)).start()
+
+                @pl.when(rel == 2)
+                def _():
+                    quarter_copy(cw_ref, q, 2, plane(1)).start()
+
+            quarter_copy(cw_ref, q, rank, mate).start()
+        for rank in range(2):
+            quarter_copy(cw_ref, 2 * (1 - g) + rank, 0, mate).wait_recv()
+
+    def x_span(c):
+        return pl.ds(pl.multiple_of(c * chunk, chunk), chunk)
+
+    def ra_copy(c):
+        return remote(
+            xp_ref.at[:, x_span(c)], ra_ref.at[:, x_span(c)], ra_send.at[c], ra_recv.at[c], (g, a, inner)
+        )
+
+    dens_ref[...] = jnp.zeros_like(dens_ref)
+
+    def products_step(c, carry):
+        t_copy(c).wait()
+        span = x_span(c)
+        c_rows = c_ref[span, :].astype(jnp.float32)
+        blocks = chunk // BLK
+        for p in range(parts):
+            masked = jnp.concatenate(
+                [
+                    t_ref[p, pl.ds(pl.multiple_of(c * chunk + j * BLK, BLK), BLK), :]
+                    * mask_ref[c * blocks + j]
+                    for j in range(blocks)
+                ],
+                axis=0,
+            )
+            prod = jnp.dot(masked, cw_ref[...], preferred_element_type=jnp.float32)
+            xp_ref[p, span, :] = prod.astype(jnp.bfloat16)
+            dens_ref[p] += jnp.sum((prod * c_rows).reshape(chunk // 8, 8, nocc), axis=0)
+
+        @pl.when(is_end)
+        def _():
+            ra_copy(c).start()
+
+        return carry
+
+    lax.fori_loop(0, CHUNKS, products_step, 0)
+
+    small = s_ref.shape[0]
+    s_ref[...] = small_ref[...]
+    tile_rows = lax.broadcasted_iota(jnp.int32, (8, 128), 0)
+    tile = jnp.zeros((8, 128), jnp.float32)
+    for p in range(parts):
+        lanes = jnp.sum(dens_ref[p], axis=0, keepdims=True)
+        folded = lanes[:, :128]
+        for j in range(1, nocc // 128):
+            folded = folded + lanes[:, j * 128 : (j + 1) * 128]
+        tile = tile + jnp.where(tile_rows == parts * g + p, folded, 0.0)
+    s_ref[small - 8 :, :] = tile
+
+    def s_copy(i):
+        device = (mate, plane(1), plane(2))[i] if i < 3 else (g, a, lax.rem(z + i - 2, 4))
+        return remote(s_ref, sr_ref.at[i], s_send.at[i], s_recv.at[i], device)
+
+    def s_start(r):
+        for i in ((0,), (1,), (2,), (3, 4, 5))[r]:
+            s_copy(i).start()
+
+    def s_finish(r):
+        batch = ((0,), (1,), (2,), (3, 4, 5))[r]
+        for i in batch:
+            s_copy(i).wait()
+        for i in batch:
+            s_ref[...] += sr_ref[i]
+
+    def rb_copy(c):
+        return remote(
+            xp_ref.at[:, x_span(c)], rb_ref.at[:, x_span(c)], rb_send.at[c], rb_recv.at[c], (g, a, 3 - z)
+        )
+
+    def xa_at(block, c):
+        return xa_ref.at[:, pl.ds(pl.multiple_of(block * rows + c * chunk, chunk), chunk)]
+
+    def xe_copy(c):
+        return remote(xa_at(a, c), xa_at(a, c), xe_send.at[c], xe_recv.at[c], (g, a, outer))
+
+    def pl_copy(c, k):
+        return remote(
+            xa_at(a, c), xa_at(a, c), pl_send.at[k - 1, c], pl_recv.at[k - 1, c], plane(k)
+        )
+
+    def pl_wait(c, k):
+        block = lax.bitwise_xor(a, k)
+        remote(
+            xa_at(block, c), xa_at(block, c), pl_send.at[k - 1, c], pl_recv.at[k - 1, c], plane(k)
+        ).wait_recv()
+
+    def xm_copy(block, c):
+        i = block * per + lax.rem(c, per)
+        dst = xm_ref.at[:, pl.ds(pl.multiple_of(i * chunk, chunk), chunk)]
+        return remote(xa_at(block, c), dst, xm_send.at[i], xm_recv.at[i], mate)
+
+    def xo_copy(c):
+        i = lax.rem(c, 2)
+        dst = xo_ref.at[:, pl.ds(pl.multiple_of(i * chunk, chunk), chunk)]
+        return remote(xa_at(a, c), dst, xo_send.at[i], xo_recv.at[i], mate)
+
+    def for_mate(c):
+        return c // per == 1 - g
+
+    def publish(c):
+        for k in (1, 2, 3):
+            pl_copy(c, k).start()
+
+        @pl.when(for_mate(c))
+        def _():
+            xm_copy(a, c).start()
+
+        @pl.when(z == c // 2)
+        def _():
+            xo_copy(c).start()
+
+    def stage_one(c):
+        ra_copy(c).wait_recv()
+        for p in range(parts):
+            both = xp_ref[p, x_span(c), :].astype(jnp.float32) + ra_ref[p, x_span(c), :].astype(jnp.float32)
+            xp_ref[p, x_span(c), :] = both.astype(jnp.bfloat16)
+        rb_copy(c).start()
+
+    def stage_two(c):
+        rb_copy(c).wait_recv()
+        for p in range(parts):
+            both = xp_ref[p, x_span(c), :].astype(jnp.float32) + rb_ref[p, x_span(c), :].astype(jnp.float32)
+            xa_ref[p, pl.ds(pl.multiple_of(a * rows + c * chunk, chunk), chunk), :] = both.astype(jnp.bfloat16)
+        xe_copy(c).start()
+        publish(c)
+
+    def slot(t):
+        @pl.when(is_mid & (t < CHUNKS))
+        def _():
+            stage_one(t)
+
+        @pl.when(is_mid & (t >= 1) & (t <= CHUNKS))
+        def _():
+            stage_two(t - 1)
+
+        @pl.when(is_end & (t >= 3))
+        def _():
+            xe_copy(t - 3).wait_recv()
+            publish(t - 3)
+
+    own_cols = pl.ds(pl.multiple_of(g * half, half), half)
+    mate_cols = pl.ds(pl.multiple_of((1 - g) * half, half), half)
+
+    def mr_copy(dest):
+        span = pl.ds(pl.multiple_of(dest * own, own), own)
+        return remote(
+            t_ref.at[0, span, mate_cols], mr_ref.at[dest], mr_send.at[dest], mr_recv.at[dest], mate
+        )
+
+    def cr_copy(k):
+        dest = lax.rem(z + k, 4)
+        span = pl.ds(pl.multiple_of(dest * own, own), own)
+        return remote(
+            t_ref.at[1, span, own_cols], cr_ref.at[z], cr_send.at[k - 1], cr_recv.at[k - 1], (g, a, dest)
+        )
+
+    def cr_wait(k):
+        src = lax.rem(z + 4 - k, 4)
+        remote(
+            t_ref.at[1, pl.ds(0, own), own_cols], cr_ref.at[src], cr_send.at[k - 1], cr_recv.at[k - 1], mate
+        ).wait_recv()
+        return src
+
+    def coulomb_part(k, d):
+        dest = lax.rem(z + k, 4)
+        step = 32
+
+        def body(i, carry):
+            row = pl.multiple_of(dest * own + i * step, step)
+            span = pl.ds(row, step)
+            total = t_ref[0, span, :].astype(jnp.float32) * d[0]
+            for p in range(1, parts):
+                total += t_ref[p, span, :].astype(jnp.float32) * d[p]
+            total = total * mask_ref[row // BLK].astype(jnp.float32)
+            t_ref[0, span, :] = total.astype(jnp.bfloat16)
+            return carry
+
+        lax.fori_loop(0, own // step, body, 0)
+        mr_copy(dest).start()
+
+    def coulomb_sum(k):
+        dest = lax.rem(z + k, 4)
+        mr_copy(dest).wait_recv()
+        step = 64
+
+        def body(i, carry):
+            span = pl.ds(pl.multiple_of(dest * own + i * step, step), step)
+            piece = pl.ds(pl.multiple_of(i * step, step), step)
+            both = t_ref[0, span, own_cols].astype(jnp.float32) + mr_ref[dest, piece, :].astype(jnp.float32)
+            if k:
+                t_ref[1, span, own_cols] = both.astype(jnp.bfloat16)
+            else:
+                cr_ref[dest, piece, :] = both.astype(jnp.bfloat16)
+            return carry
+
+        lax.fori_loop(0, own // step, body, 0)
+        if k:
+            cr_copy(k).start()
+
+    s_start(0)
+    slot(0)
+    s_finish(0)
+    s_start(1)
+    s_finish(1)
+    s_start(2)
+    slot(1)
+    s_finish(2)
+    s_start(3)
+    slot(2)
+    s_finish(3)
+    sums_ref[...] = s_ref[...]
+    dens_tile = s_ref[small - 8 :, :]
+    d = []
+    for p in range(parts):
+        row = jnp.where(tile_rows == parts * g + p, dens_tile, 0.0)
+        value = 2.0 * jnp.sum(jnp.sum(row, axis=1, keepdims=True), axis=0, keepdims=True)
+        d.append(value.astype(jnp.bfloat16).astype(jnp.float32))
+    order = (2, 1, 3, 0)
+    slot(3)
+    coulomb_part(order[0], d)
+    for i in range(1, 4):
+        coulomb_part(order[i], d)
+        coulomb_sum(order[i - 1])
+        slot(3 + i)
+    coulomb_sum(order[3])
+    for t in range(7, CHUNKS + 3):
+        slot(t)
+
+    def arrive(c, carry):
+        for k in (1, 2, 3):
+            pl_wait(c, k)
+
+            @pl.when(for_mate(c))
+            def _():
+                xm_copy(lax.bitwise_xor(a, k), c).start()
+
+        return carry
+
+    lax.fori_loop(0, CHUNKS, arrive, 0)
+
+    for i in range(2):
+        xo_copy(i).wait_recv()
+    dims = (((1,), (1,)), ((), ()))
+    own_rows = pl.ds(pl.multiple_of(a * rows + z * own, own), own)
+
+    def exchange(block, carry):
+        def body(j, inside):
+            i = block * per + j
+            xm_copy(block, j).wait_recv()
+            total = jnp.zeros((own, chunk), jnp.float32)
+            near = pl.ds(pl.multiple_of(block * rows + g * half + j * chunk, chunk), chunk)
+            far = pl.ds(pl.multiple_of(i * chunk, chunk), chunk)
+            for p in range(parts):
+                total += lax.dot_general(
+                    xa_ref[p, own_rows, :], xa_ref[p, near, :], dims, preferred_element_type=jnp.float32
+                )
+                total += lax.dot_general(
+                    xo_ref[p], xm_ref[p, far, :], dims, preferred_element_type=jnp.float32
+                )
+            eb_ref[block, :, pl.ds(pl.multiple_of(j * chunk, chunk), chunk)] = (-0.5 * total).astype(jnp.bfloat16)
+            return inside
+
+        return lax.fori_loop(0, per, body, carry)
+
+    lax.fori_loop(0, 4, exchange, 0)
+
+    def out_cols(block, core):
+        return pl.ds(pl.multiple_of(block * cols + core * half, half), half)
+
+    def om_copy(block):
+        return remote(
+            eb_ref.at[block], out_ref.at[:, out_cols(block, g)], om_send.at[block], om_recv.at[block], mate
+        )
+
+    def ol_copy(block):
+        return pltpu.make_async_copy(eb_ref.at[block], out_ref.at[:, out_cols(block, g)], ol_sem.at[block])
+
+    for k in (0, 1, 3, 2):
+        src = cr_wait(k) if k else z
+        step = 64
+
+        def body(i, carry):
+            piece = pl.ds(pl.multiple_of(i * step, step), step)
+            both = eb_ref[src, piece, :].astype(jnp.float32) + cr_ref[src, piece, :].astype(jnp.float32)
+            eb_ref[src, piece, :] = both.astype(jnp.bfloat16)
+            return carry
+
+        lax.fori_loop(0, own // step, body, 0)
+        om_copy(src).start()
+        ol_copy(src).start()
+
+    for block in range(4):
+        remote(
+            eb_ref.at[block], out_ref.at[:, out_cols(block, 1 - g)], om_send.at[block], om_recv.at[block], mate
+        ).wait()
+        ol_copy(block).wait()
+        mr_copy(block).wait_send()
+    for k in (1, 2, 3):
+        cr_copy(k).wait_send()
+
+    @pl.when(rel == 0)
+    def _():
+        for i in range(4):
+            quarter_copy(c_ref, first, i, mate).wait_send()
+
+    @pl.when(rel != 0)
+    def _():
+        for i in range(2):
+            quarter_copy(cw_ref, first, i, mate).wait_send()
+
+    @pl.when((rel == 1) | (rel == 2))
+    def _():
+        quarter_copy(cw_ref, first, 2, mate).wait_send()
+
+    def drain(c, carry):
+        @pl.when(is_end)
+        def _():
+            ra_copy(c).wait_send()
+
+        @pl.when(is_mid)
+        def _():
+            rb_copy(c).wait_send()
+            xe_copy(c).wait_send()
+
+        for k in (1, 2, 3):
+            pl_copy(c, k).wait_send()
+
+        @pl.when(for_mate(c))
+        def _():
+            for block in range(4):
+                xm_copy(block, c).wait_send()
+
+        return carry
+
+    lax.fori_loop(0, CHUNKS, drain, 0)
+    for i in range(2):
+        xo_copy(i).wait_send()
+
+
+def grid_call(fitted, mask_rows, own_c, small):
+    parts, rows, cols = fitted.shape
+    nocc = own_c.shape[1]
+    own, half = rows // 4, cols // 2
+    bf16, f32 = jnp.bfloat16, jnp.float32
+    vmem = pl.BlockSpec(memory_space=pltpu.VMEM)
+    hbm = pl.BlockSpec(memory_space=pl.ANY)
+    dma = pltpu.SemaphoreType.DMA
+    return pl.pallas_call(
+        grid_kernel,
+        in_specs=[hbm, vmem, vmem, vmem],
+        out_specs=[hbm, vmem],
+        out_shape=[
+            jax.ShapeDtypeStruct((own, 4 * cols), bf16),
+            jax.ShapeDtypeStruct(small.shape, f32),
+        ],
+        scratch_shapes=[
+            pltpu.VMEM((parts, rows, cols), bf16),
+            pltpu.VMEM((cols, nocc), bf16),
+            pltpu.VMEM((parts, rows, nocc), bf16),
+            pltpu.VMEM((parts, rows, nocc), bf16),
+            pltpu.VMEM((parts, rows, nocc), bf16),
+            pltpu.VMEM((parts, 4 * rows, nocc), bf16),
+            pltpu.VMEM((parts, 2 * rows, nocc), bf16),
+            pltpu.VMEM((parts, own, nocc), bf16),
+            pltpu.VMEM((4, own, half), bf16),
+            pltpu.VMEM((4, own, half), bf16),
+            pltpu.VMEM((4, own, half), bf16),
+            pltpu.VMEM(small.shape, f32),
+            pltpu.VMEM((6,) + small.shape, f32),
+            pltpu.VMEM((parts, 8, nocc), f32),
+            dma((CHUNKS,)),
+            dma((4,)), dma((4,)),
+            dma((CHUNKS,)), dma((CHUNKS,)),
+            dma((CHUNKS,)), dma((CHUNKS,)),
+            dma((CHUNKS,)), dma((CHUNKS,)),
+            dma((3, CHUNKS)), dma((3, CHUNKS)),
+            dma((2 * CHUNKS,)), dma((2 * CHUNKS,)),
+            dma((2,)), dma((2,)),
+            dma((6,)), dma((6,)),
+            dma((4,)), dma((4,)),
+            dma((3,)), dma((3,)),
+            dma((4,)), dma((4,)),
+            dma((4,)),
+        ],
+        compiler_params=pltpu.CompilerParams(
+            collective_id=0, has_side_effects=True, vmem_limit_bytes=GRID_VMEM
+        ),
+        cost_estimate=pl.CostEstimate(
+            flops=2 * parts * rows * cols * nocc + 8 * parts * own * 2 * cols * nocc,
+            bytes_accessed=2 * parts * rows * cols + 8 * own * cols,
+            transcendentals=0,
+        ),
+        name="grid",
+    )(fitted, mask_rows, own_c, small)
+
+
+def per_device_grid(
+    fitted_tensor, block_mask, orbitals, nuclear, centres, mm_positions, mm_charges, neighbours
+):
+    parts, row_span, col_span = fitted_tensor.shape
+    grp_id = lax.axis_index("grp")
+    aux_id = lax.axis_index("aux")
+    orb_id = lax.axis_index("orb")
+    own_span = row_span // 4
+    block_total = block_mask.shape[1]
+    row_start = aux_id * row_span
+    bits = lax.dynamic_slice(
+        block_mask[0],
+        (row_start // BLK, orb_id * (col_span // BLK)),
+        (row_span // BLK, col_span // BLK),
+    ).astype(jnp.bfloat16)
+    mask_rows = jnp.repeat(bits, BLK, axis=1)[:, None, :]
+
+    own_float = orbitals.astype(jnp.float32)
+    population = 2.0 * jnp.sum(own_float * own_float, axis=1)
+    population = jnp.where((grp_id == 0) & (orb_id == 0), population, 0.0)
+    population = lax.dynamic_update_slice(
+        jnp.zeros((block_total, BLK), jnp.float32),
+        population.reshape(row_span // BLK, BLK),
+        (aux_id * (row_span // BLK), 0),
+    )
+    centre_blocks = centres.reshape(3, block_total, BLK)
+    picker = (neighbours[0][:, None] == jnp.arange(block_total, dtype=jnp.int32)[None, :]).astype(
+        jnp.float32
+    )
+    kernel = near_kernel(picker, centre_blocks, mm_positions)
+    contrib = jnp.dot(kernel, mm_charges, precision=lax.Precision.HIGHEST).reshape(
+        picker.shape[0], BLK
+    )
+    field_part = jnp.dot(picker.T, contrib, precision=lax.Precision.HIGHEST)
+    small = jnp.concatenate([field_part, population, jnp.zeros((8, BLK), jnp.float32)], axis=0)
+
+    fock16, sums = grid_call(fitted_tensor, mask_rows, orbitals, small)
+
+    own_first = row_start + orb_id * own_span
+    field_vec = sums[:block_total].reshape(-1)
+    field_own = lax.dynamic_slice_in_dim(field_vec, own_first, own_span, 0)
+    row_ids = own_first + lax.broadcasted_iota(jnp.int32, fock16.shape, 0)
+    col_ids = lax.broadcasted_iota(jnp.int32, fock16.shape, 1)
+    fock = fock16.astype(jnp.float32) + jnp.where(row_ids == col_ids, field_own[:, None], 0.0)
+
+    charge_blocks = nuclear.reshape(block_total, BLK) - sums[block_total : 2 * block_total]
+    near_q = jnp.dot(picker, charge_blocks, precision=lax.Precision.HIGHEST).reshape(-1)
+    mm_potential = jnp.dot(near_q, kernel, precision=lax.Precision.HIGHEST)
+    return (fock, mm_potential)
+
+
+def grid_fits(mesh, fitted_tensor, orbitals):
+    shape = mesh.shape
+    parts = fitted_tensor.shape[0] // shape["grp"]
+    rows = fitted_tensor.shape[1] // shape["aux"]
+    cols = fitted_tensor.shape[2] // shape["orb"]
+    return (
+        shape["grp"] == 2
+        and shape["aux"] == 4
+        and shape["orb"] == 4
+        and parts == 2
+        and rows == cols
+        and rows % (CHUNKS * BLK) == 0
+        and orbitals.shape[1] % BLK == 0
+        and 7 * rows * cols + 41 * rows * orbitals.shape[1] <= 52 * 2**20
+    )
+
+
 def solution(mesh):
     in_specs = (
         P("grp", "aux", "orb"),
@@ -300,6 +848,13 @@
         P(("grp", "aux", "orb"), None),
     )
     out_specs = (P(("aux", "orb"), None), P(("grp", "aux", "orb")))
-    return jax.shard_map(
-        per_device, mesh=mesh, in_specs=in_specs, out_specs=out_specs, check_vma=False
-    )
+    def build(body):
+        return jax.shard_map(
+            body, mesh=mesh, in_specs=in_specs, out_specs=out_specs, check_vma=False
+        )
+
+    def run(fitted_tensor, block_mask, orbitals, *rest):
+        body = per_device_grid if grid_fits(mesh, fitted_tensor, orbitals) else per_device
+        return build(body)(fitted_tensor, block_mask, orbitals, *rest)
+
+    return run

time: 377 us -> 269 us (0.71)
  Pallas kernels: 48.6 us -> 241 us
  waiting for transfers between devices: 176 us -> 0 us
  blocking collectives: 108 us -> 0 us
  between operations: 14.4 us -> 0.74 us
  starting transfers between devices: 10.9 us -> 0 us
  other arithmetic: 8.52 us -> 18 us
    pallas_call x6 -> x1, Pallas kernels: 48.6 us -> 241 us  [grid_call(): pl.pallas_call(grid_kernel, in_specs=[hbm, vmem, vmem, vmem], out_specs=[...]
    ppermute x18 -> x0, waiting for transfers between devices: 142 us -> none  [the longest x3 126 us: per_device(): mine[k] = lax.ppermute(both, 'orb', moves[k]) if k else both]
    psum x1 -> x0, blocking collectives: 63.9 us -> none  [per_device(): lax.psum(jnp.concatenate([field_part, dens_slots], axis=0), ('grp', 'aux'...]
    all_gather x1 -> x0, blocking collectives: 44.5 us -> none  [per_device(): population = lax.all_gather(own_population, 'aux', axis=0, tiled=True)]
    all_gather x1 -> x0, waiting for transfers between devices: 34.7 us -> none  [per_device(): x_all = lax.all_gather(x_own, ('aux', 'orb'), axis=1, tiled=True)]
    add x0 -> x2, other arithmetic: none -> 13.7 us  [the longest x1 13.7 us: per_device_grid(): fock16.astype(jnp.float32)]
    ppermute x18 -> x0, starting transfers between devices: 10.9 us -> none  [the longest x3 4.21 us: per_device(): arrived.append(lax.ppermute(block, 'orb', moves[k]))]
    convert_element_type x6 -> x1, other arithmetic: 5.99 us -> 0.79 us  [per_device_grid(): bits = lax.dynamic_slice(block_mask[0], (row_start // BLK, orb_id * (col_...]
  transfers between devices with their start and end apart: 19 -> 0, of which waited for: 6 -> 0; matrix products, arithmetic and copies ran while one was open for 3% -> 0% of each run, Pallas kernels for 4% -> 0%
where the time goes in v1:
time: 269 us; the launch traced here: 267 us
  Pallas kernels  241 us (90%)
  other arithmetic  18 us (7%)
  matrix products  5.23 us (2%)
    pallas_call x1, Pallas kernels, grid_call(): pl.pallas_call(grid_kernel, in_specs=[hbm, vmem, vmem, vmem], out_specs=[...  241 us
    add x1, other arithmetic, per_device_grid(): fock16.astype(jnp.float32)  13.7 us

profile of v1, /device:TPU:0, one launch (start us, length us, event | category | flops | bytes accessed | tf_op | source)
XLA Modules:
  0.0 267.3 jit_solution(4870298128569183721)
XLA Ops:
  0.6 0.0 copy-start
  0.7 0.6 copy-done
  1.3 0.8 fusion.8
  2.1 1.1 convolution_bitcast_fusion
  3.3 1.6 multiply_reduce_fusion.1
  4.9 0.1 broadcast_in_dim.28
  5.0 0.7 broadcast_in_dim_reshape.5.mask_ref
  5.7 1.2 multiply_reduce_fusion
  6.8 1.0 fusion.1
  7.8 1.0 fusion.10
  8.8 0.7 maximum_maximum_fusion.small_ref
  9.5 0.0 copy-start.1
  9.5 0.0 copy-start.2
  9.5 241.0 %grid.1 = (bf16[512,8192]{1,0:T(8,128)(2,1)}, f32[136,128]{1,0:T(8,128)}) custom-call(bf16[2,2048,2048]{2,1,0:T(8,128)(2,1)} %t_hbm.1, bf16[16,1,2048]{2,1,0:T(2,128)(2,1)} %broadcast_in_dim_reshape.5.mask_ref, bf16[2048,256]{1,0:T(8,128)(2,1)} %c_ref.1, f32[136,128]{1,0:T(8,128)} %maximum_maximum_fusion.small_ref), custom_call_target="tpu_custom_call" | custom-call | flops 12884901888 | bytes 25165824 | tf_op jit(solution)/shard_map/grid/pallas_call | solution.py:722
  250.5 0.0 copy-done.1
  250.5 0.0 copy-done.2
  250.5 0.9 fusion.6
  251.5 0.8 slice_bitcast_fusion
  252.2 0.1 dynamic_slice.7
  252.3 1.3 fusion
  253.6 13.7 %select_add_fusion = f32[512,8192]{1,0:T(8,128)} fusion(bf16[512,8192]{1,0:T(8,128)(2,1)} %get-tuple-element.4, f32[512]{0:T(512)S(1)} %dynamic_slice.7, s32[512]{0:T(512)S(1)} %iota_add_fusion), kind=kLoop, calls=%fused_computation | loop fusion | flops 16777216 | bytes 25169920 | tf_op jit(solution)/shard_map/add | solution.py:814
  (6 shorter events, 0.0 us)
Async XLA Ops:
  0.6 0.7 copy-start
  9.5 241.0 %copy-start.1 = (f32[8192]{0:T(1024)S(1)}, f32[8192]{0:T(1024)}, u32[]{:S(2)}) copy-start(f32[8192]{0:T(1024)} %param.11) | copy-start | bytes 98308
  9.5 241.0 %copy-start.2 = (s32[1,2]{1,0:T(1,128)S(1)}, s32[1,2]{1,0:T(1,128)}, u32[]{:S(2)}) copy-start(s32[1,2]{1,0:T(1,128)} %param.15) | copy-start | bytes 28

commit v2 on v1

--- a/solution.py
+++ b/solution.py
@@ -290,6 +290,7 @@
 
 MESH = pl.DeviceIdType.MESH
 CHUNKS = 8
+AHEAD = 2
 GRID_VMEM = 58 * 1024 * 1024
 
 
@@ -401,7 +402,7 @@
             xp_ref[p, span, :] = prod.astype(jnp.bfloat16)
             dens_ref[p] += jnp.sum((prod * c_rows).reshape(chunk // 8, 8, nocc), axis=0)
 
-        @pl.when(is_end)
+        @pl.when(is_end & (c < AHEAD))
         def _():
             ra_copy(c).start()
 
@@ -498,19 +499,37 @@
         xe_copy(c).start()
         publish(c)
 
-    def slot(t):
-        @pl.when(is_mid & (t < CHUNKS))
-        def _():
-            stage_one(t)
-
-        @pl.when(is_mid & (t >= 1) & (t <= CHUNKS))
-        def _():
-            stage_two(t - 1)
-
-        @pl.when(is_end & (t >= 3))
+    def late_slot(t):
+        if t == CHUNKS:
+
+            @pl.when(is_mid)
+            def _():
+                stage_two(t - 1)
+
+        @pl.when(is_end)
         def _():
             xe_copy(t - 3).wait_recv()
             publish(t - 3)
+
+    def slot(t):
+        if t >= CHUNKS:
+            late_slot(t)
+            return
+
+        @pl.when(is_mid)
+        def _():
+            stage_one(t)
+            if t >= 1:
+                stage_two(t - 1)
+
+        @pl.when(is_end)
+        def _():
+            ra_copy(t).wait_send()
+            if t < CHUNKS - AHEAD:
+                ra_copy(t + AHEAD).start()
+            if t >= 3:
+                xe_copy(t - 3).wait_recv()
+                publish(t - 3)
 
     own_cols = pl.ds(pl.multiple_of(g * half, half), half)
     mate_cols = pl.ds(pl.multiple_of((1 - g) * half, half), half)
@@ -568,18 +587,16 @@
             return carry
 
         lax.fori_loop(0, own // step, body, 0)
-        if k:
-            cr_copy(k).start()
 
     s_start(0)
-    slot(0)
     s_finish(0)
     s_start(1)
+    slot(0)
     s_finish(1)
     s_start(2)
-    slot(1)
     s_finish(2)
     s_start(3)
+    slot(1)
     slot(2)
     s_finish(3)
     sums_ref[...] = s_ref[...]
@@ -597,8 +614,22 @@
         coulomb_sum(order[i - 1])
         slot(3 + i)
     coulomb_sum(order[3])
-    for t in range(7, CHUNKS + 3):
-        slot(t)
+    slot(7)
+
+    @pl.when(is_end)
+    def _():
+        for k in order[:3]:
+            cr_copy(k).start()
+
+    slot(8)
+
+    @pl.when(is_mid)
+    def _():
+        for k in order[:3]:
+            cr_copy(k).start()
+
+    slot(9)
+    slot(10)
 
     def arrive(c, carry):
         for k in (1, 2, 3):
@@ -687,10 +718,6 @@
         quarter_copy(cw_ref, first, 2, mate).wait_send()
 
     def drain(c, carry):
-        @pl.when(is_end)
-        def _():
-            ra_copy(c).wait_send()
-
         @pl.when(is_mid)
         def _():
             rb_copy(c).wait_send()

time: 269 us -> 220 us (0.82)
  Pallas kernels: 241 us -> 191 us
    pallas_call x1, Pallas kernels: 241 us -> 191 us  [grid_call(): pl.pallas_call(grid_kernel, in_specs=[hbm, vmem, vmem, vmem], out_specs=[...]
where the time goes in v2:
time: 220 us; the launch traced here: 217 us
  Pallas kernels  191 us (87%)
  other arithmetic  18 us (8%)
  matrix products  5.23 us (2%)
  local copies, waits for them, and re-layouts  2.31 us (1%)
    pallas_call x1, Pallas kernels, grid_call(): pl.pallas_call(grid_kernel, in_specs=[hbm, vmem, vmem, vmem], out_specs=[...  191 us
    add x1, other arithmetic, per_device_grid(): fock16.astype(jnp.float32)  13.7 us

profile of v2, /device:TPU:0, one launch (start us, length us, event | category | flops | bytes accessed | tf_op | source)
XLA Modules:
  0.0 216.9 jit_solution(6750756940711102736)
XLA Ops:
  0.6 0.0 copy-start
  0.7 0.6 copy-done
  1.3 0.8 fusion.8
  2.1 1.1 convolution_bitcast_fusion
  3.3 1.6 multiply_reduce_fusion.1
  4.9 0.1 broadcast_in_dim.28
  5.0 0.7 broadcast_in_dim_reshape.5.mask_ref
  5.7 1.2 multiply_reduce_fusion
  6.8 1.0 fusion.1
  7.8 1.0 fusion.10
  8.8 0.7 maximum_maximum_fusion.small_ref
  9.5 0.0 copy-start.1
  9.5 0.0 copy-start.2
  9.5 190.7 %grid.1 = (bf16[512,8192]{1,0:T(8,128)(2,1)}, f32[136,128]{1,0:T(8,128)}) custom-call(bf16[2,2048,2048]{2,1,0:T(8,128)(2,1)} %t_hbm.1, bf16[16,1,2048]{2,1,0:T(2,128)(2,1)} %broadcast_in_dim_reshape.5.mask_ref, bf16[2048,256]{1,0:T(8,128)(2,1)} %c_ref.1, f32[136,128]{1,0:T(8,128)} %maximum_maximum_fusion.small_ref), custom_call_target="tpu_custom_call" | custom-call | flops 12884901888 | bytes 25165824 | tf_op jit(solution)/shard_map/grid/pallas_call | solution.py:749
  200.2 0.0 copy-done.1
  200.2 0.0 copy-done.2
  200.2 0.9 fusion.6
  201.1 0.8 slice_bitcast_fusion
  201.9 0.1 dynamic_slice.7
  202.0 1.3 fusion
  203.2 13.7 %select_add_fusion = f32[512,8192]{1,0:T(8,128)} fusion(bf16[512,8192]{1,0:T(8,128)(2,1)} %get-tuple-element.4, f32[512]{0:T(512)S(1)} %dynamic_slice.7, s32[512]{0:T(512)S(1)} %iota_add_fusion), kind=kLoop, calls=%fused_computation | loop fusion | flops 16777216 | bytes 25169920 | tf_op jit(solution)/shard_map/add | solution.py:841
  (6 shorter events, 0.0 us)
Async XLA Ops:
  0.6 0.7 copy-start
  9.5 190.7 %copy-start.1 = (f32[8192]{0:T(1024)S(1)}, f32[8192]{0:T(1024)}, u32[]{:S(2)}) copy-start(f32[8192]{0:T(1024)} %param.11) | copy-start | bytes 98308
  9.5 190.7 %copy-start.2 = (s32[1,2]{1,0:T(1,128)S(1)}, s32[1,2]{1,0:T(1,128)}, u32[]{:S(2)}) copy-start(s32[1,2]{1,0:T(1,128)} %param.15) | copy-start | bytes 28

commit v3 on v2

--- a/solution.py
+++ b/solution.py
@@ -295,8 +295,9 @@
 
 
 def grid_kernel(
-    t_hbm, mask_ref, c_ref, small_ref, out_ref, sums_ref,
-    t_ref, cw_ref, xp_ref, ra_ref, rb_ref, xa_ref, xm_ref, xo_ref, mr_ref, cr_ref, eb_ref,
+    t_hbm, bits_ref, c_ref, nuclear_ref, centres_ref, place_ref, charge_ref, near_ref,
+    out_ref, potential_ref,
+    t_ref, mask_ref, kern_ref, cw_ref, xp_ref, ra_ref, rb_ref, xa_ref, xm_ref, xo_ref, mr_ref, cr_ref, eb_ref,
     s_ref, sr_ref, dens_ref,
     t_sem, c_send, c_recv, ra_send, ra_recv, rb_send, rb_recv, xe_send, xe_recv,
     pl_send, pl_recv, xm_send, xm_recv, xo_send, xo_recv, s_send, s_recv,
@@ -355,6 +356,61 @@
         quarter_copy(c_ref, first, 3, plane(2)).start()
         cw_ref[...] = c_ref[...]
 
+    row_blocks, block_total = rows // BLK, bits_ref.shape[1]
+    picked = lax.broadcasted_iota(jnp.int32, (block_total, cols), 1) // BLK + z * (cols // BLK)
+    picked = (lax.broadcasted_iota(jnp.int32, (block_total, cols), 0) == picked).astype(jnp.float32)
+    bits = bits_ref[0, pl.ds(pl.multiple_of(a * row_blocks, row_blocks), row_blocks), :].astype(jnp.float32)
+    wide = jnp.dot(
+        bits.astype(jnp.bfloat16), picked.astype(jnp.bfloat16), preferred_element_type=jnp.float32
+    )
+    for j in range(row_blocks):
+        mask_ref[j] = wide[j : j + 1, :].astype(jnp.bfloat16)
+
+    eye = lax.broadcasted_iota(jnp.int32, (BLK, BLK), 0) == lax.broadcasted_iota(jnp.int32, (BLK, BLK), 1)
+
+    def to_row(column):
+        return jnp.sum(jnp.where(eye, column, 0.0), axis=0, keepdims=True)
+
+    def to_column(row):
+        return jnp.sum(jnp.where(eye, row, 0.0), axis=1, keepdims=True)
+
+    s_ref[...] = jnp.zeros_like(s_ref)
+    share = jnp.where((g == 0) & (z == 0), 2.0, 0.0)
+
+    def population_step(j, carry):
+        block = c_ref[pl.ds(pl.multiple_of(j * BLK, BLK), BLK), :].astype(jnp.float32)
+        row = to_row(jnp.sum(block * block, axis=1, keepdims=True))
+        s_ref[pl.ds(block_total + a * row_blocks + j, 1), :] = share * row
+        return carry
+
+    lax.fori_loop(0, row_blocks, population_step, 0)
+
+    near_count = near_ref.shape[1]
+    block_ids = lax.broadcasted_iota(jnp.int32, (block_total, BLK), 0)
+    for k in range(near_count):
+        near_id = near_ref[:, k : k + 1]
+        near_xyz = jnp.zeros((3, BLK), jnp.float32)
+        for b in range(block_total):
+            near_xyz = near_xyz + jnp.where(near_id == b, centres_ref[:, b * BLK : (b + 1) * BLK], 0.0)
+        squares = None
+        for axis in range(3):
+            offset = to_column(near_xyz[axis : axis + 1, :]) - place_ref[axis : axis + 1, :]
+            squares = offset * offset if squares is None else squares + offset * offset
+        kern = lax.rsqrt(squares + softening)
+        kern_ref[k] = kern
+        contrib = to_row(jnp.sum(kern * charge_ref[...], axis=1, keepdims=True))
+        s_ref[:block_total, :] += jnp.where(block_ids == near_id, contrib, 0.0)
+
+    def potentials():
+        charges = nuclear_ref[...] - s_ref[block_total : 2 * block_total, :]
+        total = jnp.zeros(potential_ref.shape, jnp.float32)
+        for k in range(near_count):
+            near_q = jnp.sum(
+                jnp.where(block_ids == near_ref[:, k : k + 1], charges, 0.0), axis=0, keepdims=True
+            )
+            total = total + jnp.sum(kern_ref[k] * to_column(near_q), axis=0, keepdims=True)
+        potential_ref[...] = total
+
     @pl.when(rel != 0)
     def _():
         for rank in range(2):
@@ -411,7 +467,6 @@
     lax.fori_loop(0, CHUNKS, products_step, 0)
 
     small = s_ref.shape[0]
-    s_ref[...] = small_ref[...]
     tile_rows = lax.broadcasted_iota(jnp.int32, (8, 128), 0)
     tile = jnp.zeros((8, 128), jnp.float32)
     for p in range(parts):
@@ -599,7 +654,6 @@
     slot(1)
     slot(2)
     s_finish(3)
-    sums_ref[...] = s_ref[...]
     dens_tile = s_ref[small - 8 :, :]
     d = []
     for p in range(parts):
@@ -609,6 +663,7 @@
     order = (2, 1, 3, 0)
     slot(3)
     coulomb_part(order[0], d)
+    potentials()
     for i in range(1, 4):
         coulomb_part(order[i], d)
         coulomb_sum(order[i - 1])
@@ -662,7 +717,16 @@
                 total += lax.dot_general(
                     xo_ref[p], xm_ref[p, far, :], dims, preferred_element_type=jnp.float32
                 )
-            eb_ref[block, :, pl.ds(pl.multiple_of(j * chunk, chunk), chunk)] = (-0.5 * total).astype(jnp.bfloat16)
+            first = jnp.where(block == a, g * half + j * chunk - z * own, -4 * rows)
+            field_row = a * row_blocks + g * (half // BLK) + j * (chunk // BLK)
+            field = jnp.concatenate(
+                [s_ref[pl.ds(field_row + i, 1), :] for i in range(chunk // BLK)], axis=1
+            )
+            diagonal = lax.broadcasted_iota(jnp.int32, (own, chunk), 0) == first + lax.broadcasted_iota(
+                jnp.int32, (own, chunk), 1
+            )
+            total = jnp.where(diagonal, field, 0.0) - 0.5 * total
+            eb_ref[block, :, pl.ds(pl.multiple_of(j * chunk, chunk), chunk)] = total.astype(jnp.bfloat16)
             return inside
 
         return lax.fori_loop(0, per, body, carry)
@@ -738,24 +802,28 @@
         xo_copy(i).wait_send()
 
 
-def grid_call(fitted, mask_rows, own_c, small):
+def grid_call(fitted, block_mask, own_c, nuclear, centres, positions, charges, neighbours):
     parts, rows, cols = fitted.shape
     nocc = own_c.shape[1]
     own, half = rows // 4, cols // 2
+    block_total = block_mask.shape[1]
+    small = (2 * block_total + 8, BLK)
     bf16, f32 = jnp.bfloat16, jnp.float32
     vmem = pl.BlockSpec(memory_space=pltpu.VMEM)
     hbm = pl.BlockSpec(memory_space=pl.ANY)
     dma = pltpu.SemaphoreType.DMA
     return pl.pallas_call(
         grid_kernel,
-        in_specs=[hbm, vmem, vmem, vmem],
+        in_specs=[hbm] + [vmem] * 7,
         out_specs=[hbm, vmem],
         out_shape=[
             jax.ShapeDtypeStruct((own, 4 * cols), bf16),
-            jax.ShapeDtypeStruct(small.shape, f32),
+            jax.ShapeDtypeStruct((1, positions.shape[1]), f32),
         ],
         scratch_shapes=[
             pltpu.VMEM((parts, rows, cols), bf16),
+            pltpu.VMEM((rows // BLK, 1, cols), bf16),
+            pltpu.VMEM((neighbours.shape[1], BLK, positions.shape[1]), f32),
             pltpu.VMEM((cols, nocc), bf16),
             pltpu.VMEM((parts, rows, nocc), bf16),
             pltpu.VMEM((parts, rows, nocc), bf16),
@@ -766,8 +834,8 @@
             pltpu.VMEM((4, own, half), bf16),
             pltpu.VMEM((4, own, half), bf16),
             pltpu.VMEM((4, own, half), bf16),
-            pltpu.VMEM(small.shape, f32),
-            pltpu.VMEM((6,) + small.shape, f32),
+            pltpu.VMEM(small, f32),
+            pltpu.VMEM((6,) + small, f32),
             pltpu.VMEM((parts, 8, nocc), f32),
             dma((CHUNKS,)),
             dma((4,)), dma((4,)),
@@ -792,58 +860,41 @@
             transcendentals=0,
         ),
         name="grid",
-    )(fitted, mask_rows, own_c, small)
+    )(
+        fitted, block_mask, own_c, nuclear.reshape(block_total, BLK), centres, positions,
+        charges.reshape(1, -1), neighbours,
+    )
+
+
+def finish_kernel(in_ref, out_ref):
+    out_ref[...] = in_ref[...].astype(jnp.float32)
+
+
+def finish_call(fock16):
+    rows, cols = fock16.shape
+    step = 64
+    spec = pl.BlockSpec((step, cols), lambda i: (i, 0))
+    return pl.pallas_call(
+        finish_kernel,
+        grid=(rows // step,),
+        in_specs=[spec],
+        out_specs=spec,
+        out_shape=jax.ShapeDtypeStruct((rows, cols), jnp.float32),
+        compiler_params=pltpu.CompilerParams(vmem_limit_bytes=VMEM_LIMIT),
+        cost_estimate=pl.CostEstimate(
+            flops=rows * cols, bytes_accessed=6 * rows * cols, transcendentals=0
+        ),
+        name="finish",
+    )(fock16)
 
 
 def per_device_grid(
     fitted_tensor, block_mask, orbitals, nuclear, centres, mm_positions, mm_charges, neighbours
 ):
-    parts, row_span, col_span = fitted_tensor.shape
-    grp_id = lax.axis_index("grp")
-    aux_id = lax.axis_index("aux")
-    orb_id = lax.axis_index("orb")
-    own_span = row_span // 4
-    block_total = block_mask.shape[1]
-    row_start = aux_id * row_span
-    bits = lax.dynamic_slice(
-        block_mask[0],
-        (row_start // BLK, orb_id * (col_span // BLK)),
-        (row_span // BLK, col_span // BLK),
-    ).astype(jnp.bfloat16)
-    mask_rows = jnp.repeat(bits, BLK, axis=1)[:, None, :]
-
-    own_float = orbitals.astype(jnp.float32)
-    population = 2.0 * jnp.sum(own_float * own_float, axis=1)
-    population = jnp.where((grp_id == 0) & (orb_id == 0), population, 0.0)
-    population = lax.dynamic_update_slice(
-        jnp.zeros((block_total, BLK), jnp.float32),
-        population.reshape(row_span // BLK, BLK),
-        (aux_id * (row_span // BLK), 0),
+    fock16, potential = grid_call(
+        fitted_tensor, block_mask, orbitals, nuclear, centres, mm_positions, mm_charges, neighbours
     )
-    centre_blocks = centres.reshape(3, block_total, BLK)
-    picker = (neighbours[0][:, None] == jnp.arange(block_total, dtype=jnp.int32)[None, :]).astype(
-        jnp.float32
-    )
-    kernel = near_kernel(picker, centre_blocks, mm_positions)
-    contrib = jnp.dot(kernel, mm_charges, precision=lax.Precision.HIGHEST).reshape(
-        picker.shape[0], BLK
-    )
-    field_part = jnp.dot(picker.T, contrib, precision=lax.Precision.HIGHEST)
-    small = jnp.concatenate([field_part, population, jnp.zeros((8, BLK), jnp.float32)], axis=0)
-
-    fock16, sums = grid_call(fitted_tensor, mask_rows, orbitals, small)
-
-    own_first = row_start + orb_id * own_span
-    field_vec = sums[:block_total].reshape(-1)
-    field_own = lax.dynamic_slice_in_dim(field_vec, own_first, own_span, 0)
-    row_ids = own_first + lax.broadcasted_iota(jnp.int32, fock16.shape, 0)
-    col_ids = lax.broadcasted_iota(jnp.int32, fock16.shape, 1)
-    fock = fock16.astype(jnp.float32) + jnp.where(row_ids == col_ids, field_own[:, None], 0.0)
-
-    charge_blocks = nuclear.reshape(block_total, BLK) - sums[block_total : 2 * block_total]
-    near_q = jnp.dot(picker, charge_blocks, precision=lax.Precision.HIGHEST).reshape(-1)
-    mm_potential = jnp.dot(near_q, kernel, precision=lax.Precision.HIGHEST)
-    return (fock, mm_potential)
+    return (finish_call(fock16), potential.reshape(-1))
 
 
 def grid_fits(mesh, fitted_tensor, orbitals):

time: 220 us -> 205 us (0.932); the launches traced: 217 us -> 205 us
  other arithmetic: 18 us -> 0 us
  Pallas kernels: 191 us -> 204 us
  matrix products: 5.23 us -> 0 us
    add x2 -> x0, other arithmetic: 13.7 us -> none  [the longest x1 13.7 us: per_device_grid(): fock16.astype(jnp.float32)]
    pallas_call x1 -> x2, Pallas kernels: 191 us -> 204 us  [the longest x1 193 us: grid_call(): pl.pallas_call(grid_kernel, in_specs=[hbm] + [vmem] * 7, out_specs=[hbm,...]
    dot_general x5 -> x0, matrix products: 5.23 us -> none  [the longest x1 1.26 us: per_device_grid(): mm_potential = jnp.dot(near_q, kernel, precision=lax.Precision.HIGHEST)]
    reduce_sum x2 -> x0, other arithmetic: 2.76 us -> none  [the longest x1 1.58 us: per_device_grid(): population = 2.0 * jnp.sum(own_float * own_float, axis=1)]
where the time goes in v3:
time: 205 us
  Pallas kernels  204 us (100%)
    pallas_call x1, Pallas kernels, grid_call(): pl.pallas_call(grid_kernel, in_specs=[hbm] + [vmem] * 7, out_specs=[hbm,...  193 us
    pallas_call x1, Pallas kernels, finish_call(): pl.pallas_call(finish_kernel, grid=(rows // step,), in_specs=[spec], out_...  10.3 us

profile of v3, /device:TPU:0, one launch (start us, length us, event | category | flops | bytes accessed | tf_op | source)
XLA Modules:
  0.0 205.0 jit_solution(16327848650288990437)
XLA Ops:
  0.6 193.4 %grid.1 = (bf16[512,8192]{1,0:T(8,128)(2,1)}, f32[1,1024]{1,0:T(1,128)}) custom-call(bf16[2,2048,2048]{2,1,0:T(8,128)(2,1)} %t_hbm.1, s32[1,64,64]{2,1,0:T(8,128)} %bits_ref.1, bf16[2048,256]{1,0:T(8,128)(2,1)} %c_ref.1, f32[64,128]{1,0:T(8,128)} %bitcast.4, f32[3,8192]{1,0:T(4,128)} %centres_ref.1, f32[3,1024]{1,0:T(4,128)} %place_ref.1, ...), custom_call_target="tpu_custom_call" | custom-call | flops 12884901888 | bytes 25165824 | tf_op jit(solution)/shard_map/grid/pallas_call | solution.py:815
  194.1 0.0 copy-start
  194.1 10.3 %finish.1 = f32[512,8192]{1,0:T(8,128)} custom-call(bf16[512,8192]{1,0:T(8,128)(2,1)} %get-tuple-element.4.in_ref), custom_call_target="tpu_custom_call" | custom-call | flops 4194304 | bytes 25165824 | tf_op jit(solution)/shard_map/finish/pallas_call | solution.py:877
  204.4 0.0 copy-done
  204.4 0.6 copy.11
Async XLA Ops:
  194.1 10.3 %copy-start = (f32[1,1024]{1,0:T(1,128)S(1)}, f32[1,1024]{1,0:T(1,128)}, u32[]{:S(2)}) copy-start(f32[1,1024]{1,0:T(1,128)} %get-tuple-element.5) | copy-start | bytes 12292

commit v4 on v3

--- a/solution.py
+++ b/solution.py
@@ -289,8 +289,11 @@
 
 
 MESH = pl.DeviceIdType.MESH
-CHUNKS = 8
+CHUNKS = 16
+STEPS = 8
 AHEAD = 2
+LAG = 4
+PIECES = 4
 GRID_VMEM = 58 * 1024 * 1024
 
 
@@ -306,7 +309,11 @@
     parts, rows, cols = t_ref.shape
     nocc = c_ref.shape[1]
     chunk = rows // CHUNKS
+    load = rows // STEPS
+    tile = 2 * BLK
     own = rows // 4
+    piece = own // PIECES
+    per_own = own // chunk
     half = cols // 2
     quarter = cols // 4
     per = CHUNKS // 2
@@ -328,10 +335,10 @@
         )
 
     def t_copy(c):
-        span = pl.ds(c * chunk, chunk)
+        span = pl.ds(c * load, load)
         return pltpu.make_async_copy(t_hbm.at[:, span], t_ref.at[:, span], t_sem.at[c])
 
-    for c in range(CHUNKS):
+    for c in range(STEPS):
         t_copy(c).start()
 
     barrier = pltpu.get_barrier_semaphore()
@@ -352,8 +359,6 @@
     def _():
         quarter_copy(c_ref, first, 0, plane(1)).start()
         quarter_copy(c_ref, second, 1, plane(2)).start()
-        quarter_copy(c_ref, second, 2, plane(1)).start()
-        quarter_copy(c_ref, first, 3, plane(2)).start()
         cw_ref[...] = c_ref[...]
 
     row_blocks, block_total = rows // BLK, bits_ref.shape[1]
@@ -373,6 +378,13 @@
 
     def to_column(row):
         return jnp.sum(jnp.where(eye, row, 0.0), axis=1, keepdims=True)
+
+    @pl.when(rel == 0)
+    def _():
+        quarter_copy(c_ref, first, 0, plane(1)).wait_send()
+        quarter_copy(c_ref, second, 2, plane(1)).start()
+        quarter_copy(c_ref, second, 1, plane(2)).wait_send()
+        quarter_copy(c_ref, first, 3, plane(2)).start()
 
     s_ref[...] = jnp.zeros_like(s_ref)
     share = jnp.where((g == 0) & (z == 0), 2.0, 0.0)
@@ -442,13 +454,13 @@
 
     def products_step(c, carry):
         t_copy(c).wait()
-        span = x_span(c)
+        span = pl.ds(pl.multiple_of(c * load, load), load)
         c_rows = c_ref[span, :].astype(jnp.float32)
-        blocks = chunk // BLK
+        blocks = load // BLK
         for p in range(parts):
             masked = jnp.concatenate(
                 [
-                    t_ref[p, pl.ds(pl.multiple_of(c * chunk + j * BLK, BLK), BLK), :]
+                    t_ref[p, pl.ds(pl.multiple_of(c * load + j * BLK, BLK), BLK), :]
                     * mask_ref[c * blocks + j]
                     for j in range(blocks)
                 ],
@@ -456,26 +468,27 @@
             )
             prod = jnp.dot(masked, cw_ref[...], preferred_element_type=jnp.float32)
             xp_ref[p, span, :] = prod.astype(jnp.bfloat16)
-            dens_ref[p] += jnp.sum((prod * c_rows).reshape(chunk // 8, 8, nocc), axis=0)
-
-        @pl.when(is_end & (c < AHEAD))
+            dens_ref[p] += jnp.sum((prod * c_rows).reshape(load // 8, 8, nocc), axis=0)
+
+        @pl.when(is_end & (c == 0))
         def _():
-            ra_copy(c).start()
+            for first_chunk in range(AHEAD):
+                ra_copy(first_chunk).start()
 
         return carry
 
-    lax.fori_loop(0, CHUNKS, products_step, 0)
+    lax.fori_loop(0, STEPS, products_step, 0)
 
     small = s_ref.shape[0]
     tile_rows = lax.broadcasted_iota(jnp.int32, (8, 128), 0)
-    tile = jnp.zeros((8, 128), jnp.float32)
+    dens_rows = jnp.zeros((8, 128), jnp.float32)
     for p in range(parts):
         lanes = jnp.sum(dens_ref[p], axis=0, keepdims=True)
         folded = lanes[:, :128]
         for j in range(1, nocc // 128):
             folded = folded + lanes[:, j * 128 : (j + 1) * 128]
-        tile = tile + jnp.where(tile_rows == parts * g + p, folded, 0.0)
-    s_ref[small - 8 :, :] = tile
+        dens_rows = dens_rows + jnp.where(tile_rows == parts * g + p, folded, 0.0)
+    s_ref[small - 8 :, :] = dens_rows
 
     def s_copy(i):
         device = (mate, plane(1), plane(2))[i] if i < 3 else (g, a, lax.rem(z + i - 2, 4))
@@ -520,7 +533,7 @@
         return remote(xa_at(block, c), dst, xm_send.at[i], xm_recv.at[i], mate)
 
     def xo_copy(c):
-        i = lax.rem(c, 2)
+        i = lax.rem(c, per_own)
         dst = xo_ref.at[:, pl.ds(pl.multiple_of(i * chunk, chunk), chunk)]
         return remote(xa_at(a, c), dst, xo_send.at[i], xo_recv.at[i], mate)
 
@@ -535,7 +548,7 @@
         def _():
             xm_copy(a, c).start()
 
-        @pl.when(z == c // 2)
+        @pl.when(z == c // per_own)
         def _():
             xo_copy(c).start()
 
@@ -563,8 +576,8 @@
 
         @pl.when(is_end)
         def _():
-            xe_copy(t - 3).wait_recv()
-            publish(t - 3)
+            xe_copy(t - LAG).wait_recv()
+            publish(t - LAG)
 
     def slot(t):
         if t >= CHUNKS:
@@ -582,9 +595,9 @@
             ra_copy(t).wait_send()
             if t < CHUNKS - AHEAD:
                 ra_copy(t + AHEAD).start()
-            if t >= 3:
-                xe_copy(t - 3).wait_recv()
-                publish(t - 3)
+            if t >= LAG:
+                xe_copy(t - LAG).wait_recv()
+                publish(t - LAG)
 
     own_cols = pl.ds(pl.multiple_of(g * half, half), half)
     mate_cols = pl.ds(pl.multiple_of((1 - g) * half, half), half)
@@ -595,22 +608,23 @@
             t_ref.at[0, span, mate_cols], mr_ref.at[dest], mr_send.at[dest], mr_recv.at[dest], mate
         )
 
-    def cr_copy(k):
-        dest = lax.rem(z + k, 4)
-        span = pl.ds(pl.multiple_of(dest * own, own), own)
+    def cr_copy(k, n):
+        dest = lax.bitwise_xor(z, k)
+        span = pl.ds(pl.multiple_of(dest * own + n * piece, piece), piece)
         return remote(
-            t_ref.at[1, span, own_cols], cr_ref.at[z], cr_send.at[k - 1], cr_recv.at[k - 1], (g, a, dest)
+            t_ref.at[1, span, own_cols], cr_ref.at[z, pl.ds(n * piece, piece)],
+            cr_send.at[k - 1, n], cr_recv.at[k - 1, n], (g, a, dest),
         )
 
-    def cr_wait(k):
-        src = lax.rem(z + 4 - k, 4)
+    def cr_wait(k, n):
+        src = lax.bitwise_xor(z, k)
         remote(
-            t_ref.at[1, pl.ds(0, own), own_cols], cr_ref.at[src], cr_send.at[k - 1], cr_recv.at[k - 1], mate
+            t_ref.at[1, pl.ds(0, piece), own_cols], cr_ref.at[src, pl.ds(n * piece, piece)],
+            cr_send.at[k - 1, n], cr_recv.at[k - 1, n], (g, a, src),
         ).wait_recv()
-        return src
 
     def coulomb_part(k, d):
-        dest = lax.rem(z + k, 4)
+        dest = lax.bitwise_xor(z, k)
         step = 32
 
         def body(i, carry):
@@ -627,18 +641,18 @@
         mr_copy(dest).start()
 
     def coulomb_sum(k):
-        dest = lax.rem(z + k, 4)
+        dest = lax.bitwise_xor(z, k)
         mr_copy(dest).wait_recv()
         step = 64
 
         def body(i, carry):
             span = pl.ds(pl.multiple_of(dest * own + i * step, step), step)
-            piece = pl.ds(pl.multiple_of(i * step, step), step)
-            both = t_ref[0, span, own_cols].astype(jnp.float32) + mr_ref[dest, piece, :].astype(jnp.float32)
+            part = pl.ds(pl.multiple_of(i * step, step), step)
+            both = t_ref[0, span, own_cols].astype(jnp.float32) + mr_ref[dest, part, :].astype(jnp.float32)
             if k:
                 t_ref[1, span, own_cols] = both.astype(jnp.bfloat16)
             else:
-                cr_ref[dest, piece, :] = both.astype(jnp.bfloat16)
+                cr_ref[dest, part, :] = both.astype(jnp.bfloat16)
             return carry
 
         lax.fori_loop(0, own // step, body, 0)
@@ -649,10 +663,11 @@
     slot(0)
     s_finish(1)
     s_start(2)
+    slot(1)
     s_finish(2)
     s_start(3)
-    slot(1)
-    slot(2)
+    for t in range(2, 7):
+        slot(t)
     s_finish(3)
     dens_tile = s_ref[small - 8 :, :]
     d = []
@@ -660,31 +675,36 @@
         row = jnp.where(tile_rows == parts * g + p, dens_tile, 0.0)
         value = 2.0 * jnp.sum(jnp.sum(row, axis=1, keepdims=True), axis=0, keepdims=True)
         d.append(value.astype(jnp.bfloat16).astype(jnp.float32))
-    order = (2, 1, 3, 0)
-    slot(3)
-    coulomb_part(order[0], d)
-    potentials()
-    for i in range(1, 4):
+    order = (2, 3, 1, 0)
+    for i in range(4):
+        slot(7 + 2 * i)
         coulomb_part(order[i], d)
-        coulomb_sum(order[i - 1])
-        slot(3 + i)
-    coulomb_sum(order[3])
-    slot(7)
+        slot(8 + 2 * i)
+        if i:
+            coulomb_sum(order[i - 1])
+    slot(15)
+    cross = [(k, n) for n in range(PIECES) for k in (2, 3)]
+
+    def coulomb_start():
+        for n in range(PIECES):
+            cr_copy(1, n).start()
+        for k, n in cross[:2]:
+            cr_copy(k, n).start()
 
     @pl.when(is_end)
     def _():
-        for k in order[:3]:
-            cr_copy(k).start()
-
-    slot(8)
+        coulomb_start()
+
+    slot(CHUNKS)
 
     @pl.when(is_mid)
     def _():
-        for k in order[:3]:
-            cr_copy(k).start()
-
-    slot(9)
-    slot(10)
+        coulomb_start()
+
+    coulomb_sum(order[3])
+    potentials()
+    for t in range(CHUNKS + 1, CHUNKS + LAG):
+        slot(t)
 
     def arrive(c, carry):
         for k in (1, 2, 3):
@@ -696,20 +716,28 @@
 
         return carry
 
-    lax.fori_loop(0, CHUNKS, arrive, 0)
-
-    for i in range(2):
+    def next_cross(q):
+        cr_copy(*cross[q - 2]).wait_send()
+        cr_copy(*cross[q]).start()
+
+    seen = 0
+    for q, until in ((2, 8), (3, 11), (4, 14), (5, CHUNKS)):
+        next_cross(q)
+        lax.fori_loop(seen, until, arrive, 0)
+        seen = until
+    next_cross(6)
+    for i in range(per_own):
         xo_copy(i).wait_recv()
     dims = (((1,), (1,)), ((), ()))
     own_rows = pl.ds(pl.multiple_of(a * rows + z * own, own), own)
 
     def exchange(block, carry):
         def body(j, inside):
-            i = block * per + j
-            xm_copy(block, j).wait_recv()
-            total = jnp.zeros((own, chunk), jnp.float32)
-            near = pl.ds(pl.multiple_of(block * rows + g * half + j * chunk, chunk), chunk)
-            far = pl.ds(pl.multiple_of(i * chunk, chunk), chunk)
+            for i in range(tile // chunk):
+                xm_copy(block, j * (tile // chunk) + i).wait_recv()
+            total = jnp.zeros((own, tile), jnp.float32)
+            near = pl.ds(pl.multiple_of(block * rows + g * half + j * tile, tile), tile)
+            far = pl.ds(pl.multiple_of(block * half + j * tile, tile), tile)
             for p in range(parts):
                 total += lax.dot_general(
                     xa_ref[p, own_rows, :], xa_ref[p, near, :], dims, preferred_element_type=jnp.float32
@@ -717,59 +745,85 @@
                 total += lax.dot_general(
                     xo_ref[p], xm_ref[p, far, :], dims, preferred_element_type=jnp.float32
                 )
-            first = jnp.where(block == a, g * half + j * chunk - z * own, -4 * rows)
-            field_row = a * row_blocks + g * (half // BLK) + j * (chunk // BLK)
+            first = jnp.where(block == a, g * half + j * tile - z * own, -4 * rows)
+            field_row = a * row_blocks + g * (half // BLK) + j * (tile // BLK)
             field = jnp.concatenate(
-                [s_ref[pl.ds(field_row + i, 1), :] for i in range(chunk // BLK)], axis=1
+                [s_ref[pl.ds(field_row + i, 1), :] for i in range(tile // BLK)], axis=1
             )
-            diagonal = lax.broadcasted_iota(jnp.int32, (own, chunk), 0) == first + lax.broadcasted_iota(
-                jnp.int32, (own, chunk), 1
+            diagonal = lax.broadcasted_iota(jnp.int32, (own, tile), 0) == first + lax.broadcasted_iota(
+                jnp.int32, (own, tile), 1
             )
             total = jnp.where(diagonal, field, 0.0) - 0.5 * total
-            eb_ref[block, :, pl.ds(pl.multiple_of(j * chunk, chunk), chunk)] = total.astype(jnp.bfloat16)
+            eb_ref[block, :, pl.ds(pl.multiple_of(j * tile, tile), tile)] = total.astype(jnp.bfloat16)
             return inside
 
-        return lax.fori_loop(0, per, body, carry)
-
-    lax.fori_loop(0, 4, exchange, 0)
+        return lax.fori_loop(0, half // tile, body, carry)
+
+    lax.fori_loop(0, 2, exchange, 0)
+    next_cross(7)
+    lax.fori_loop(2, 4, exchange, 0)
 
     def out_cols(block, core):
         return pl.ds(pl.multiple_of(block * cols + core * half, half), half)
 
-    def om_copy(block):
+    def piece_at(n):
+        return pl.ds(pl.multiple_of(n * piece, piece), piece)
+
+    def om_copy(block, n, core):
         return remote(
-            eb_ref.at[block], out_ref.at[:, out_cols(block, g)], om_send.at[block], om_recv.at[block], mate
+            eb_ref.at[block, piece_at(n)], out_ref.at[piece_at(n), out_cols(block, core)],
+            om_send.at[block, n], om_recv.at[block, n], mate,
         )
 
-    def ol_copy(block):
-        return pltpu.make_async_copy(eb_ref.at[block], out_ref.at[:, out_cols(block, g)], ol_sem.at[block])
-
-    for k in (0, 1, 3, 2):
-        src = cr_wait(k) if k else z
+    def ol_copy(block, n):
+        return pltpu.make_async_copy(
+            eb_ref.at[block, piece_at(n)], out_ref.at[piece_at(n), out_cols(block, g)], ol_sem.at[block, n]
+        )
+
+    def finish_piece(block, n):
         step = 64
 
         def body(i, carry):
-            piece = pl.ds(pl.multiple_of(i * step, step), step)
-            both = eb_ref[src, piece, :].astype(jnp.float32) + cr_ref[src, piece, :].astype(jnp.float32)
-            eb_ref[src, piece, :] = both.astype(jnp.bfloat16)
+            part = pl.ds(pl.multiple_of(n * piece + i * step, step), step)
+            both = eb_ref[block, part, :].astype(jnp.float32) + cr_ref[block, part, :].astype(jnp.float32)
+            eb_ref[block, part, :] = both.astype(jnp.bfloat16)
             return carry
 
-        lax.fori_loop(0, own // step, body, 0)
-        om_copy(src).start()
-        ol_copy(src).start()
-
-    for block in range(4):
-        remote(
-            eb_ref.at[block], out_ref.at[:, out_cols(block, 1 - g)], om_send.at[block], om_recv.at[block], mate
-        ).wait()
-        ol_copy(block).wait()
+        lax.fori_loop(0, piece // step, body, 0)
+        om_copy(block, n, g).start()
+        ol_copy(block, n).start()
+
+    def finish_near(n, carry):
+        finish_piece(z, n)
+        cr_wait(1, n)
+        finish_piece(lax.bitwise_xor(z, 1), n)
+        return carry
+
+    lax.fori_loop(0, PIECES, finish_near, 0)
+
+    def finish_cross(n, carry):
+        for k in (2, 3):
+            cr_wait(k, n)
+            finish_piece(lax.bitwise_xor(z, k), n)
+        return carry
+
+    lax.fori_loop(0, PIECES, finish_cross, 0)
+
+    for k, n in cross[-2:] + [(1, n) for n in range(PIECES)]:
+        cr_copy(k, n).wait_send()
+
+    def drain_out(block, carry):
+        for n in range(PIECES):
+            om_copy(block, n, 1 - g).wait()
+            ol_copy(block, n).wait()
         mr_copy(block).wait_send()
-    for k in (1, 2, 3):
-        cr_copy(k).wait_send()
+        return carry
+
+    lax.fori_loop(0, 4, drain_out, 0)
 
     @pl.when(rel == 0)
     def _():
-        for i in range(4):
+        for i in range(2, 4):
             quarter_copy(c_ref, first, i, mate).wait_send()
 
     @pl.when(rel != 0)
@@ -798,7 +852,7 @@
         return carry
 
     lax.fori_loop(0, CHUNKS, drain, 0)
-    for i in range(2):
+    for i in range(per_own):
         xo_copy(i).wait_send()
 
 
@@ -837,19 +891,19 @@
             pltpu.VMEM(small, f32),
             pltpu.VMEM((6,) + small, f32),
             pltpu.VMEM((parts, 8, nocc), f32),
-            dma((CHUNKS,)),
+            dma((STEPS,)),
             dma((4,)), dma((4,)),
             dma((CHUNKS,)), dma((CHUNKS,)),
             dma((CHUNKS,)), dma((CHUNKS,)),
             dma((CHUNKS,)), dma((CHUNKS,)),
             dma((3, CHUNKS)), dma((3, CHUNKS)),
             dma((2 * CHUNKS,)), dma((2 * CHUNKS,)),
-            dma((2,)), dma((2,)),
+            dma((own * CHUNKS // rows,)), dma((own * CHUNKS // rows,)),
             dma((6,)), dma((6,)),
             dma((4,)), dma((4,)),
-            dma((3,)), dma((3,)),
-            dma((4,)), dma((4,)),
-            dma((4,)),
+            dma((3, PIECES)), dma((3, PIECES)),
+            dma((4, PIECES)), dma((4, PIECES)),
+            dma((4, PIECES)),
         ],
         compiler_params=pltpu.CompilerParams(
             collective_id=0, has_side_effects=True, vmem_limit_bytes=GRID_VMEM
@@ -909,6 +963,7 @@
         and parts == 2
         and rows == cols
         and rows % (CHUNKS * BLK) == 0
+        and rows % (2 * STEPS * BLK) == 0
         and orbitals.shape[1] % BLK == 0
         and 7 * rows * cols + 41 * rows * orbitals.shape[1] <= 52 * 2**20
     )

time: 205 us -> 187 us (0.912)
  Pallas kernels: 204 us -> 185 us
    pallas_call x1, Pallas kernels: 193 us -> 175 us  [grid_call(): pl.pallas_call(grid_kernel, in_specs=[hbm] + [vmem] * 7, out_specs=[hbm,...]
where the time goes in v4:
time: 187 us; the launch traced here: 186 us
  Pallas kernels  185 us (99%)
    pallas_call x1, Pallas kernels, grid_call(): pl.pallas_call(grid_kernel, in_specs=[hbm] + [vmem] * 7, out_specs=[hbm,...  175 us
    pallas_call x1, Pallas kernels, finish_call(): pl.pallas_call(finish_kernel, grid=(rows // step,), in_specs=[spec], out_...  10.3 us

profile of v4, /device:TPU:0, one launch (start us, length us, event | category | flops | bytes accessed | tf_op | source)
XLA Modules:
  0.0 186.1 jit_solution(2461007524479532397)
XLA Ops:
  0.6 174.6 %grid.1 = (bf16[512,8192]{1,0:T(8,128)(2,1)}, f32[1,1024]{1,0:T(1,128)}) custom-call(bf16[2,2048,2048]{2,1,0:T(8,128)(2,1)} %t_hbm.1, s32[1,64,64]{2,1,0:T(8,128)} %bits_ref.1, bf16[2048,256]{1,0:T(8,128)(2,1)} %c_ref.1, f32[64,128]{1,0:T(8,128)} %bitcast.4, f32[3,8192]{1,0:T(4,128)} %centres_ref.1, f32[3,1024]{1,0:T(4,128)} %place_ref.1, ...), custom_call_target="tpu_custom_call" | custom-call | flops 12884901888 | bytes 25165824 | tf_op jit(solution)/shard_map/grid/pallas_call | solution.py:869
  175.2 0.0 copy-start
  175.2 10.3 %finish.1 = f32[512,8192]{1,0:T(8,128)} custom-call(bf16[512,8192]{1,0:T(8,128)(2,1)} %get-tuple-element.4.in_ref), custom_call_target="tpu_custom_call" | custom-call | flops 4194304 | bytes 25165824 | tf_op jit(solution)/shard_map/finish/pallas_call | solution.py:931
  185.5 0.0 copy-done
  185.5 0.6 copy.11
Async XLA Ops:
  175.2 10.3 %copy-start = (f32[1,1024]{1,0:T(1,128)S(1)}, f32[1,1024]{1,0:T(1,128)}, u32[]{:S(2)}) copy-start(f32[1,1024]{1,0:T(1,128)} %get-tuple-element.5) | copy-start | bytes 12292

commit v5 on v4

--- a/solution.py
+++ b/solution.py
@@ -294,6 +294,7 @@
 AHEAD = 2
 LAG = 4
 PIECES = 4
+FLIGHT = 4
 GRID_VMEM = 58 * 1024 * 1024
 
 
@@ -470,9 +471,10 @@
             xp_ref[p, span, :] = prod.astype(jnp.bfloat16)
             dens_ref[p] += jnp.sum((prod * c_rows).reshape(load // 8, 8, nocc), axis=0)
 
-        @pl.when(is_end & (c == 0))
-        def _():
-            for first_chunk in range(AHEAD):
+        for first_chunk in range(AHEAD):
+
+            @pl.when(is_end & (c == 3 * first_chunk))
+            def _():
                 ra_copy(first_chunk).start()
 
         return carry
@@ -666,7 +668,7 @@
     slot(1)
     s_finish(2)
     s_start(3)
-    for t in range(2, 7):
+    for t in range(2, 5):
         slot(t)
     s_finish(3)
     dens_tile = s_ref[small - 8 :, :]
@@ -676,19 +678,23 @@
         value = 2.0 * jnp.sum(jnp.sum(row, axis=1, keepdims=True), axis=0, keepdims=True)
         d.append(value.astype(jnp.bfloat16).astype(jnp.float32))
     order = (2, 3, 1, 0)
+    work = {}
     for i in range(4):
-        slot(7 + 2 * i)
-        coulomb_part(order[i], d)
-        slot(8 + 2 * i)
-        if i:
-            coulomb_sum(order[i - 1])
+        work.setdefault(5 + 2 * i, []).append((coulomb_part, (order[i], d)))
+        if i < 3:
+            work.setdefault(5 + 2 * i + 3, []).append((coulomb_sum, (order[i],)))
+    for t in range(5, CHUNKS - 1):
+        for act, given in work.get(t, ()):
+            act(*given)
+        slot(t)
+    for t in range(CHUNKS - 1, CHUNKS + 6):
+        for act, given in work.get(t, ()):
+            act(*given)
     slot(15)
     cross = [(k, n) for n in range(PIECES) for k in (2, 3)]
 
     def coulomb_start():
-        for n in range(PIECES):
-            cr_copy(1, n).start()
-        for k, n in cross[:2]:
+        for k, n in cross[:FLIGHT]:
             cr_copy(k, n).start()
 
     @pl.when(is_end)
@@ -706,6 +712,9 @@
     for t in range(CHUNKS + 1, CHUNKS + LAG):
         slot(t)
 
+    for n in range(PIECES):
+        cr_copy(1, n).start()
+
     def arrive(c, carry):
         for k in (1, 2, 3):
             pl_wait(c, k)
@@ -717,11 +726,11 @@
         return carry
 
     def next_cross(q):
-        cr_copy(*cross[q - 2]).wait_send()
+        cr_copy(*cross[q - FLIGHT]).wait_send()
         cr_copy(*cross[q]).start()
 
     seen = 0
-    for q, until in ((2, 8), (3, 11), (4, 14), (5, CHUNKS)):
+    for q, until in ((4, 13), (5, CHUNKS)):
         next_cross(q)
         lax.fori_loop(seen, until, arrive, 0)
         seen = until
@@ -809,7 +818,7 @@
 
     lax.fori_loop(0, PIECES, finish_cross, 0)
 
-    for k, n in cross[-2:] + [(1, n) for n in range(PIECES)]:
+    for k, n in cross[-FLIGHT:] + [(1, n) for n in range(PIECES)]:
         cr_copy(k, n).wait_send()
 
     def drain_out(block, carry):
@@ -920,20 +929,49 @@
     )
 
 
-def finish_kernel(in_ref, out_ref):
-    out_ref[...] = in_ref[...].astype(jnp.float32)
+def finish_kernel(in_hbm, out_hbm, in_ref, out_ref, in_sem, out_sem):
+    pieces = in_sem.shape[0]
+    rows = in_ref.shape[0] // pieces
+
+    def load(n):
+        span = pl.ds(pl.multiple_of(n * rows, rows), rows)
+        return pltpu.make_async_copy(in_hbm.at[span], in_ref.at[span], in_sem.at[n])
+
+    def save(n):
+        span = pl.ds(pl.multiple_of(n * rows, rows), rows)
+        return pltpu.make_async_copy(out_ref.at[span], out_hbm.at[span], out_sem.at[n])
+
+    for n in range(pieces):
+        load(n).start()
+
+    def widen(n, carry):
+        load(n).wait()
+        for r in range(rows // 16):
+            span = pl.ds(pl.multiple_of(n * rows + r * 16, 16), 16)
+            out_ref[span, :] = in_ref[span, :].astype(jnp.float32)
+        save(n).start()
+        return carry
+
+    lax.fori_loop(0, pieces, widen, 0)
+    for n in range(pieces):
+        save(n).wait()
 
 
 def finish_call(fock16):
     rows, cols = fock16.shape
-    step = 64
-    spec = pl.BlockSpec((step, cols), lambda i: (i, 0))
+    pieces = rows // 32
+    hbm = pl.BlockSpec(memory_space=pl.ANY)
     return pl.pallas_call(
         finish_kernel,
-        grid=(rows // step,),
-        in_specs=[spec],
-        out_specs=spec,
+        in_specs=[hbm],
+        out_specs=hbm,
         out_shape=jax.ShapeDtypeStruct((rows, cols), jnp.float32),
+        scratch_shapes=[
+            pltpu.VMEM((rows, cols), jnp.bfloat16),
+            pltpu.VMEM((rows, cols), jnp.float32),
+            pltpu.SemaphoreType.DMA((pieces,)),
+            pltpu.SemaphoreType.DMA((pieces,)),
+        ],
         compiler_params=pltpu.CompilerParams(vmem_limit_bytes=VMEM_LIMIT),
         cost_estimate=pl.CostEstimate(
             flops=rows * cols, bytes_accessed=6 * rows * cols, transcendentals=0

time: 187 us -> 185 us (0.989)
    pallas_call x1, Pallas kernels: 10.3 us -> 8.22 us  [finish_call(): pl.pallas_call(finish_kernel, in_specs=[hbm], out_specs=hbm, out_shape=ja...]
where the time goes in v5:
time: 185 us
  Pallas kernels  184 us (99%)
    pallas_call x1, Pallas kernels, grid_call(): pl.pallas_call(grid_kernel, in_specs=[hbm] + [vmem] * 7, out_specs=[hbm,...  175 us
    pallas_call x1, Pallas kernels, finish_call(): pl.pallas_call(finish_kernel, in_specs=[hbm], out_specs=hbm, out_shape=ja...  8.22 us

profile of v5, /device:TPU:0, one launch (start us, length us, event | category | flops | bytes accessed | tf_op | source)
XLA Modules:
  0.0 184.8 jit_solution(5686586900651153603)
XLA Ops:
  0.6 175.3 %grid.1 = (bf16[512,8192]{1,0:T(8,128)(2,1)}, f32[1,1024]{1,0:T(1,128)}) custom-call(bf16[2,2048,2048]{2,1,0:T(8,128)(2,1)} %t_hbm.1, s32[1,64,64]{2,1,0:T(8,128)} %bits_ref.1, bf16[2048,256]{1,0:T(8,128)(2,1)} %c_ref.1, f32[64,128]{1,0:T(8,128)} %bitcast.4, f32[3,8192]{1,0:T(4,128)} %centres_ref.1, f32[3,1024]{1,0:T(4,128)} %place_ref.1, ...), custom_call_target="tpu_custom_call" | custom-call | flops 12884901888 | bytes 25165824 | tf_op jit(solution)/shard_map/grid/pallas_call | solution.py:878
  175.9 0.0 copy-start
  175.9 8.2 %finish.1 = f32[512,8192]{1,0:T(8,128)} custom-call(bf16[512,8192]{1,0:T(8,128)(2,1)} %get-tuple-element.4.in_hbm), custom_call_target="tpu_custom_call" | custom-call | flops 4194304 | bytes 25165824 | tf_op jit(solution)/shard_map/finish/pallas_call | solution.py:964
  184.2 0.0 copy-done
  184.2 0.6 copy.11
Async XLA Ops:
  175.9 8.2 %copy-start = (f32[1,1024]{1,0:T(1,128)S(1)}, f32[1,1024]{1,0:T(1,128)}, u32[]{:S(2)}) copy-start(f32[1,1024]{1,0:T(1,128)} %get-tuple-element.5) | copy-start | bytes 12292
